TPU v7x, 512 devices: a whole 4x4x16 slice. The times are simulated.
512 devices in a mesh: mode: 8 (over y, core), col: 64 (over z, x).
Axes of the slice: x: 4, y: 4, z: 16, core: 2. Of those that a mesh axis runs over, the one named last changes fastest.
Arguments:
- tensor: float32 [512, 64, 4096], P('mode', 'col'), may hold values from -15 to 15
- start_basis: float32 [512, 128], replicated, may hold values from -6 to 6
Outputs:
- factor: float32 [512, 512], replicated
- basis: float32 [512, 128], replicated
- core: float32 [128, 64, 4096], P(None, 'col', 'mode')
All inputs are finite; a program needn't handle non-finite values.
Results may differ from a plain program's by a relative error of at most 0.00018.
Values sent between devices are 32-bit elements; how exact they have to be, the bound alone decides.
No kernel may reach another device: no remote copies, remote signals or barrier semaphores. Data moves between devices by JAX's collectives and lax.ppermute only.
A program may use at most 64 MiB of HBM per device.

v0:
```python
import jax
import jax.numpy as jnp
from jax import lax
from jax.sharding import PartitionSpec as P

POWER = 2


def matmul(left, right):
    return jnp.dot(left, right, precision=lax.Precision.HIGHEST, preferred_element_type=jnp.float32)


def orthonormal(image):
    small = jnp.linalg.cholesky(matmul(image.T, image))
    return jax.scipy.linalg.solve_triangular(small, image.T, lower=True).T


def per_device(tensor, start_basis):
    regrouped = lax.all_to_all(tensor, "mode", split_axis=2, concat_axis=0, tiled=True)
    rows = regrouped.shape[0]
    flat = regrouped.reshape(rows, -1)
    columns = flat.shape[1] * lax.axis_size("mode") * lax.axis_size("col")
    gram = matmul(flat, flat.T)
    total = lax.psum(gram, ("mode", "col"))
    factor = jnp.linalg.cholesky(total / columns)
    basis = start_basis
    for step in range(POWER):
        image = matmul(factor, matmul(factor.T, basis))
        basis = orthonormal(image)
    core = matmul(basis.T, flat).reshape(basis.shape[1], regrouped.shape[1], regrouped.shape[2])
    return (factor, basis, core)


def solution(mesh):
    in_specs = (P("mode", "col", None), P())
    out_specs = (P(), P(), P(None, "col", "mode"))
    return jax.shard_map(
        per_device, mesh=mesh, in_specs=in_specs, out_specs=out_specs, check_vma=False
    )
```

profile of v0, /device:TPU:1, one launch (start us, length us, event | category | flops | bytes accessed | tf_op | source)
XLA Modules:
  0.0 693.0 jit_solution(17729864730392221940)
XLA Ops:
  7.2 4.4 copy.33
  12.1 19.4 %reduce.28 = f32[4096,64]{1,0:T(8,128)} reduce(f32[4096,1,64]{2,1,0:T(1,128)S(1)} %bitcast.73, f32[]{:T(128)} %broadcast.200), dimensions={1}, to_apply=%bitcast.49.reduce_sub_computation | reduce | bytes 2097156
  31.5 2.6 reshape.50
  34.1 24.4 %all_to_all.15 = f32[8,1,32768]{2,1,0:T(1,128)S(1)} all-to-all(f32[8,1,32768]{2,1,0:T(1,128)S(1)} %reshape.50), channel_id=1, replica_groups=mesh['mode'=8,'col'=64] {'mode'}, dimensions={0} | all-to-all | bytes 2097152 | tf_op jit(solution)/shard_map/all_to_all | solution.py:19
  58.4 3.1 reduce.29
  61.6 2.6 reshape.51
  64.2 1.8 copy.43
  65.9 1.8 copy.35
  67.8 2.8 fusion.22
  70.6 466.2 %all-reduce.3.cloned.1.call-done = f32[512,512]{0,1:T(8,128)} async-done(((f32[512,512]{0,1:T(8,128)}), f32[512,512]{0,1:T(8,128)}) %all-reduce.3.cloned.1.call-update) | async-done | bytes 1048592 | tf_op jit(solution)/shard_map/psum | solution.py:24
  536.8 2.4 broadcast_multiply_fusion
  539.2 1.6 copy.37
  542.0 11.9 %cholesky.120 = f32[128,128]{1,0:T(8,128)S(1)} custom-call(f32[128,128]{1,0:T(8,128)S(1)} %cholesky.330), custom_call_target="Cholesky" | custom-call | tf_op jit(solution)/shard_map/jit(cholesky)/cholesky | solution.py:25
  553.9 9.8 %custom-call.32 = f32[1,128,128]{1,2,0:T(8,128)S(1)} custom-call(f32[1,128,128]{2,1,0:T(8,128)S(1)} %get-tuple-element.29), custom_call_target="InvertDiagBlocksLowerTriangular" | custom-call | tf_op jit(solution)/shard_map/jit(cholesky)/cholesky | solution.py:25
  563.8 1.2 constant_dynamic-update-slice_fusion.2
  565.1 1.3 convolution_subtract_fusion
  566.3 11.7 %cholesky.244 = f32[128,128]{1,0:T(8,128)S(1)} custom-call(f32[128,128]{1,0:T(8,128)S(1)} %cholesky.334), custom_call_target="Cholesky" | custom-call | tf_op jit(solution)/shard_map/jit(cholesky)/cholesky | solution.py:25
  578.1 9.8 %custom-call.33 = f32[1,128,128]{1,2,0:T(8,128)S(1)} custom-call(f32[1,128,128]{2,1,0:T(8,128)S(1)} %get-tuple-element.26), custom_call_target="InvertDiagBlocksLowerTriangular" | custom-call | tf_op jit(solution)/shard_map/jit(cholesky)/cholesky | solution.py:25
  588.2 1.3 convolution_subtract_fusion.1
  589.5 11.9 %cholesky.265 = f32[128,128]{1,0:T(8,128)S(1)} custom-call(f32[128,128]{1,0:T(8,128)S(1)} %cholesky.339), custom_call_target="Cholesky" | custom-call | tf_op jit(solution)/shard_map/jit(cholesky)/cholesky | solution.py:25
  602.2 9.8 %custom-call.34 = f32[1,128,128]{1,2,0:T(8,128)S(1)} custom-call(f32[1,128,128]{2,1,0:T(8,128)S(1)} %get-tuple-element.23), custom_call_target="InvertDiagBlocksLowerTriangular" | custom-call | tf_op jit(solution)/shard_map/jit(cholesky)/cholesky | solution.py:25
  612.2 1.2 convolution_subtract_fusion.2
  613.4 11.7 %cholesky.282 = f32[128,128]{1,0:T(8,128)S(1)} custom-call(f32[128,128]{1,0:T(8,128)S(1)} %convolution_subtract_fusion.2), custom_call_target="Cholesky" | custom-call | tf_op jit(solution)/shard_map/jit(cholesky)/cholesky | solution.py:25
  629.2 1.8 fusion.23
  631.0 1.0 fusion.24
  632.8 12.1 %cholesky.310 = f32[128,128]{1,0:T(8,128)S(1)} custom-call(f32[128,128]{1,0:T(8,128)S(1)} %fusion.18), custom_call_target="Cholesky" | custom-call | tf_op jit(solution)/shard_map/jit(cholesky)/cholesky | solution.py:14
  646.2 9.8 %custom-call.36 = f32[1,128,128]{1,2,0:T(8,128)S(1)} custom-call(f32[1,128,128]{2,1,0:T(8,128)S(1)} %fusion.11), custom_call_target="InvertDiagBlocksLowerTriangular" | custom-call | tf_op jit(solution)/shard_map/jit(_solve_triangular)/triangular_solve | solution.py:15
  656.4 1.8 fusion.26
  658.3 1.0 fusion.27
  660.0 11.9 %cholesky.321 = f32[128,128]{1,0:T(8,128)S(1)} custom-call(f32[128,128]{1,0:T(8,128)S(1)} %fusion.16), custom_call_target="Cholesky" | custom-call | tf_op jit(solution)/shard_map/jit(cholesky)/cholesky | solution.py:14
  673.2 9.8 %custom-call.37 = f32[1,128,128]{1,2,0:T(8,128)S(1)} custom-call(f32[1,128,128]{2,1,0:T(8,128)S(1)} %fusion.12), custom_call_target="InvertDiagBlocksLowerTriangular" | custom-call | tf_op jit(solution)/shard_map/jit(_solve_triangular)/triangular_solve | solution.py:15
  684.1 1.0 copy.41
  (42 shorter events, 11.1 us)
Async XLA Ops:
  7.2 622.1 %copy-start = (f32[512,128]{1,0:T(8,128)S(1)}, f32[512,128]{1,0:T(8,128)}, u32[]{:S(2)}) copy-start(f32[512,128]{1,0:T(8,128)} %param.6) | copy-start | bytes 786436
  7.2 529.6 %all-reduce.3.cloned.1.call-start = ((), (), s32[]{:S(2)}) async-start(), calls=%async_computation.1 | async-start | bytes 2097152 | tf_op jit(solution)/shard_map/psum | solution.py:24
  536.8 3.9 copy-start.2
  541.0 1.0 copy-start.3
  629.2 29.0 %copy-start.1 = (f32[512,512]{1,0:T(8,128)}, f32[512,512]{1,0:T(8,128)S(1)}, u32[]{:S(2)}) copy-start(f32[512,512]{1,0:T(8,128)S(1)} %select_select_fusion) | copy-start | bytes 3145732
Sparse Core Ops, SparseCore 0:
  70.8 466.0 all-reduce.2
where the time goes:
time: 698 us; the launch traced here: 693 us
  waiting for transfers between devices  466 us (67%)
  other arithmetic  150 us (21%)
  blocking collectives  24.4 us (3%)
  local copies, waits for them, and re-layouts  18.3 us (3%)
  between operations  17.2 us (2%)
  matrix products  16.6 us (2%)
    psum x1, waiting for transfers between devices, per_device(): total = lax.psum(gram, ('mode', 'col'))  466 us
    another operation x14, other arithmetic, per_device(): factor = jnp.linalg.cholesky(total / columns)  78.8 us
    another operation x6, other arithmetic, orthonormal(): small = jnp.linalg.cholesky(matmul(image.T, image))  25.3 us
    all_to_all x1, blocking collectives, per_device(): lax.all_to_all(tensor, 'mode', split_axis=2, concat_axis=0, tiled=True)  24.4 us
    another operation x4, other arithmetic, orthonormal(): return jax.scipy.linalg.solve_triangular(small, image.T, lower=True).T  20.9 us
    unnamed x1, other arithmetic  19.4 us
  transfers between devices with their start and end apart: 1, of which 1 were waited for; matrix products, arithmetic and copies ran while one was open for 0% of the time, Pallas kernels for 0%

commit v1 on v0

v1 whole, which is shorter than its diff:
```python
import jax
import jax.numpy as jnp
from jax import lax
from jax.experimental import pallas as pl
from jax.experimental.pallas import tpu as pltpu
from jax.sharding import Mesh, PartitionSpec as P

POWER = 2
LANES = 128
BLOCKS = [(r, c) for r in range(4) for c in range(r + 1)]


def matmul(left, right):
    return jnp.dot(left, right, precision=lax.Precision.HIGHEST, preferred_element_type=jnp.float32)


def orthonormal(image):
    small = jnp.linalg.cholesky(matmul(image.T, image))
    return jax.scipy.linalg.solve_triangular(small, image.T, lower=True).T


def split_kernel(x_ref, o_ref):
    for d in range(8):
        for c in range(4):
            o_ref[d, :, c * LANES : (c + 1) * LANES] = x_ref[pl.ds(d * 4 + c, 64, stride=32), :]


def split_columns(tensor):
    flat = tensor.reshape(64 * 32, LANES)
    return pl.pallas_call(
        split_kernel,
        out_shape=jax.ShapeDtypeStruct((8, 64, 512), jnp.float32),
    )(flat)


def dot_t(left, right):
    return lax.dot_general(left, right, (((1,), (1,)), ((), ())), preferred_element_type=jnp.float32)


def gram_kernel(f_ref, o_ref):
    full = f_ref[...]
    high = full.astype(jnp.bfloat16)
    low = (full - high.astype(jnp.float32)).astype(jnp.bfloat16)
    for r in range(4):
        rows = slice(r * LANES, (r + 1) * LANES)
        n = (r + 1) * LANES
        part = dot_t(high[rows], high[:n]) + dot_t(high[rows], low[:n]) + dot_t(low[rows], high[:n])
        for c in range(r + 1):
            start = BLOCKS.index((r, c)) * LANES
            o_ref[start : start + LANES, :] = part[:, c * LANES : (c + 1) * LANES]


def packed_gram(flat):
    return pl.pallas_call(
        gram_kernel,
        out_shape=jax.ShapeDtypeStruct((len(BLOCKS) * LANES, LANES), jnp.float32),
    )(flat)


def total_sum(packed):
    rows = packed.shape[0]
    own = lax.all_to_all(packed.reshape(32, rows // 32, LANES), ("mode", "x"), 0, 0, tiled=True).sum(0)
    own = jnp.pad(own, ((0, 8), (0, 0))).reshape(16, 3, LANES)
    own = lax.all_to_all(own, "z", 0, 0, tiled=True).sum(0)
    own = lax.all_to_all(jnp.broadcast_to(own, (16, 3, LANES)), "z", 0, 0, tiled=True)
    own = own.reshape(48, LANES)[: rows // 32]
    own = lax.all_to_all(jnp.broadcast_to(own, (32, *own.shape)), ("mode", "x"), 0, 0, tiled=True)
    return own.reshape(rows, LANES)


def unpack(packed):
    blocks = {b: packed[i * LANES : (i + 1) * LANES] for i, b in enumerate(BLOCKS)}
    return jnp.block([[blocks[(r, c)] if r >= c else blocks[(c, r)].T for c in range(4)] for r in range(4)])


def per_device(tensor, start_basis):
    regrouped = lax.all_to_all(split_columns(tensor), "mode", 0, 0, tiled=True)
    flat = regrouped.reshape(512, 512)
    scaled = unpack(total_sum(packed_gram(flat))) / 262144
    factor = jnp.linalg.cholesky(scaled)
    basis = start_basis
    for step in range(POWER):
        basis = orthonormal(matmul(scaled, basis))
    core = matmul(basis.T, flat).reshape(128, 1, 512)
    return (factor, basis, core)


def solution(mesh):
    grid = Mesh(mesh.devices.reshape(8, 16, 4), ("mode", "z", "x"))
    in_specs = (P("mode", ("z", "x"), None), P())
    out_specs = (P(), P(), P(None, ("z", "x"), "mode"))
    return jax.shard_map(
        per_device, mesh=grid, in_specs=in_specs, out_specs=out_specs, check_vma=False
    )
```

time: 698 us -> 253 us (0.36)
  waiting for transfers between devices: 466 us -> 0 us
  blocking collectives: 24.4 us -> 99.4 us
  other arithmetic: 150 us -> 127 us
  between operations: 17.2 us -> 3.84 us
  local copies, waits for them, and re-layouts: 18.3 us -> 5.46 us
  matrix products: 16.6 us -> 8.2 us
    psum x1 -> x0, waiting for transfers between devices: 466 us -> none  [per_device(): total = lax.psum(gram, ('mode', 'col'))]
    all_to_all x1 -> x5, blocking collectives: 24.4 us -> 99.4 us  [the longest x1 26.1 us: per_device(): regrouped = lax.all_to_all(split_columns(tensor), 'mode', 0, 0, tiled=True)]
    unnamed x1 -> x0, other arithmetic: 19.4 us -> none
    unnamed x14 -> x18, local copies, waits for them, and re-layouts: 12.8 us -> 4.3 us
    another operation x14 -> x15, other arithmetic: 78.8 us -> 79.5 us  [per_device(): factor = jnp.linalg.cholesky(scaled)]
  transfers between devices with their start and end apart: 1 -> 0, of which waited for: 1 -> 0; matrix products, arithmetic and copies ran while one was open for 0% -> 0% of each run, Pallas kernels for 0% -> 0%
where the time goes in v1:
time: 253 us; the launch traced here: 250 us
  other arithmetic  127 us (50%)
  blocking collectives  99.4 us (39%)
  matrix products  8.2 us (3%)
  Pallas kernels  6.22 us (2%)
  local copies, waits for them, and re-layouts  5.46 us (2%)
  between operations  3.84 us (2%)
    another operation x15, other arithmetic, per_device(): factor = jnp.linalg.cholesky(scaled)  79.5 us
    all_to_all x1, blocking collectives, per_device(): regrouped = lax.all_to_all(split_columns(tensor), 'mode', 0, 0, tiled=True)  26.1 us
    another operation x6, other arithmetic, orthonormal(): small = jnp.linalg.cholesky(matmul(image.T, image))  24.8 us
    all_to_all x1, blocking collectives, total_sum(): own = lax.all_to_all(own, 'z', 0, 0, tiled=True).sum(0)  22.6 us
    another operation x4, other arithmetic, orthonormal(): return jax.scipy.linalg.solve_triangular(small, image.T, lower=True).T  21.1 us
    all_to_all x1, blocking collectives, total_sum(): lax.all_to_all(jnp.broadcast_to(own, (32, *own.shape)), ('mode', 'x'), 0,...  19.4 us
    all_to_all x1, blocking collectives, total_sum(): lax.all_to_all(packed.reshape(32, rows // 32, LANES), ('mode', 'x'), 0, 0...  17.2 us
    all_to_all x1, blocking collectives, total_sum(): lax.all_to_all(jnp.broadcast_to(own, (16, 3, LANES)), 'z', 0, 0, tiled=True)  14 us

profile of v1, /device:TPU:1, one launch (start us, length us, event | category | flops | bytes accessed | tf_op | source)
XLA Modules:
  0.0 249.9 jit_solution(14462984054017294859)
XLA Ops:
  0.6 2.8 %shard_map.49 = f32[8,64,512]{2,1,0:T(8,128)} custom-call(f32[2048,128]{1,0:T(8,128)} %bitcast.79), custom_call_target="tpu_custom_call" | custom-call | tf_op jit(solution)/shard_map/pallas_call | solution.py:30
  3.5 26.1 %all_to_all.25 = f32[8,64,512]{2,1,0:T(8,128)} all-to-all(f32[8,64,512]{2,1,0:T(8,128)} %shard_map.49), channel_id=1, replica_groups=mesh['mode'=8,'z'=16,'x'=4] {'mode'}, dimensions={0} | all-to-all | bytes 2097152 | tf_op jit(solution)/shard_map/all_to_all | solution.py:77
  29.6 3.4 %shard_map.50 = f32[1280,128]{1,0:T(8,128)} custom-call(f32[512,512]{1,0:T(8,128)} %bitcast.71), custom_call_target="tpu_custom_call" | custom-call | tf_op jit(solution)/shard_map/pallas_call | solution.py:54
  33.0 17.2 %all_to_all.26 = f32[32,40,128]{2,1,0:T(8,128)S(1)} all-to-all(f32[32,40,128]{2,1,0:T(8,128)} %bitcast.74), channel_id=1, replica_groups=mesh['mode'=8,'z'=16,'x'=4] {'mode','x'}, dimensions={0} | all-to-all | bytes 1310720 | tf_op jit(solution)/shard_map/all_to_all | solution.py:62
  50.3 22.6 %all_to_all.27 = f32[16,3,128]{2,1,0:T(4,128)S(1)} all-to-all(f32[16,3,128]{2,1,0:T(4,128)S(1)} %reshape.65), channel_id=1, replica_groups=mesh['mode'=8,'z'=16,'x'=4] {'z'}, dimensions={0} | all-to-all | bytes 49152 | tf_op jit(solution)/shard_map/all_to_all | solution.py:64
  72.9 14.0 %all_to_all.28 = f32[16,3,128]{2,1,0:T(4,128)S(1)} all-to-all(f32[16,3,128]{2,1,0:T(4,128)S(1)} %broadcast_in_dim.9), channel_id=1, replica_groups=mesh['mode'=8,'z'=16,'x'=4] {'z'}, dimensions={0} | all-to-all | bytes 49152 | tf_op jit(solution)/shard_map/all_to_all | solution.py:65
  87.0 19.4 %all_to_all.29 = f32[32,40,128]{2,1,0:T(8,128)S(1)} all-to-all(f32[32,40,128]{2,1,0:T(8,128)S(1)} %broadcast_in_dim.10), channel_id=1, replica_groups=mesh['mode'=8,'z'=16,'x'=4] {'mode','x'}, dimensions={0} | all-to-all | bytes 1310720 | tf_op jit(solution)/shard_map/all_to_all | solution.py:67
  108.2 1.0 copy-done.2
  109.1 11.7 %cholesky.120 = f32[128,128]{1,0:T(8,128)S(1)} custom-call(f32[128,128]{1,0:T(8,128)S(1)} %cholesky.330), custom_call_target="Cholesky" | custom-call | tf_op jit(solution)/shard_map/jit(cholesky)/cholesky | solution.py:80
  121.0 1.8 fusion.23
  123.5 11.7 %cholesky.310 = f32[128,128]{1,0:T(8,128)S(1)} custom-call(f32[128,128]{1,0:T(8,128)S(1)} %fusion.18), custom_call_target="Cholesky" | custom-call | tf_op jit(solution)/shard_map/jit(cholesky)/cholesky | solution.py:18
  135.3 0.6 compare_reduce_fusion.1
  135.9 0.7 fusion.11
  136.6 9.9 %custom-call.36 = f32[1,128,128]{1,2,0:T(8,128)S(1)} custom-call(f32[1,128,128]{2,1,0:T(8,128)S(1)} %fusion.11), custom_call_target="InvertDiagBlocksLowerTriangular" | custom-call | tf_op jit(solution)/shard_map/jit(_solve_triangular)/triangular_solve | solution.py:19
  147.0 1.8 fusion.25
  149.5 11.7 %cholesky.321 = f32[128,128]{1,0:T(8,128)S(1)} custom-call(f32[128,128]{1,0:T(8,128)S(1)} %fusion.16), custom_call_target="Cholesky" | custom-call | tf_op jit(solution)/shard_map/jit(cholesky)/cholesky | solution.py:18
  161.3 0.6 compare_reduce_fusion
  161.9 0.7 fusion.12
  162.6 9.8 %custom-call.37 = f32[1,128,128]{1,2,0:T(8,128)S(1)} custom-call(f32[1,128,128]{2,1,0:T(8,128)S(1)} %fusion.12), custom_call_target="InvertDiagBlocksLowerTriangular" | custom-call | tf_op jit(solution)/shard_map/jit(_solve_triangular)/triangular_solve | solution.py:19
  172.8 0.7 convolution_bitcast_fusion
  173.6 1.0 copy.32
  174.5 1.8 copy.31
  176.3 10.0 %custom-call.32 = f32[1,128,128]{1,2,0:T(8,128)S(1)} custom-call(f32[1,128,128]{2,1,0:T(8,128)S(1)} %get-tuple-element.32), custom_call_target="InvertDiagBlocksLowerTriangular" | custom-call | tf_op jit(solution)/shard_map/jit(cholesky)/cholesky | solution.py:80
  187.0 11.7 %cholesky.244 = f32[128,128]{1,0:T(8,128)S(1)} custom-call(f32[128,128]{1,0:T(8,128)S(1)} %cholesky.334), custom_call_target="Cholesky" | custom-call | tf_op jit(solution)/shard_map/jit(cholesky)/cholesky | solution.py:80
  198.7 0.7 compare_reduce_fusion.4
  200.1 9.8 %custom-call.33 = f32[1,128,128]{1,2,0:T(8,128)S(1)} custom-call(f32[1,128,128]{2,1,0:T(8,128)S(1)} %get-tuple-element.29), custom_call_target="InvertDiagBlocksLowerTriangular" | custom-call | tf_op jit(solution)/shard_map/jit(cholesky)/cholesky | solution.py:80
  210.6 11.9 %cholesky.265 = f32[128,128]{1,0:T(8,128)S(1)} custom-call(f32[128,128]{1,0:T(8,128)S(1)} %cholesky.339), custom_call_target="Cholesky" | custom-call | tf_op jit(solution)/shard_map/jit(cholesky)/cholesky | solution.py:80
  222.6 0.6 compare_reduce_fusion.3
  223.2 9.8 %custom-call.34 = f32[1,128,128]{1,2,0:T(8,128)S(1)} custom-call(f32[1,128,128]{2,1,0:T(8,128)S(1)} %get-tuple-element.26), custom_call_target="InvertDiagBlocksLowerTriangular" | custom-call | tf_op jit(solution)/shard_map/jit(cholesky)/cholesky | solution.py:80
  233.6 11.7 %cholesky.282 = f32[128,128]{1,0:T(8,128)S(1)} custom-call(f32[128,128]{1,0:T(8,128)S(1)} %convolution_subtract_fusion.2), custom_call_target="Cholesky" | custom-call | tf_op jit(solution)/shard_map/jit(cholesky)/cholesky | solution.py:80
  245.4 0.7 compare_reduce_fusion.2
  248.6 1.1 select_select_fusion
  (56 shorter events, 6.9 us)
Async XLA Ops:
  0.6 120.4 %copy-start = (f32[512,128]{1,0:T(8,128)S(1)}, f32[512,128]{1,0:T(8,128)}, u32[]{:S(2)}) copy-start(f32[512,128]{1,0:T(8,128)} %param.6) | copy-start | bytes 786436
  108.2 1.0 copy-start.2
  148.8 24.0 %copy-start.1 = (f32[8,64,512]{2,1,0:T(8,128)S(1)}, f32[8,64,512]{2,1,0:T(8,128)}, u32[]{:S(2)}) copy-start(f32[8,64,512]{2,1,0:T(8,128)} %all_to_all.25) | copy-start | bytes 3145732
  172.8 0.7 copy-start.4
  172.8 13.5 %copy-start.3 = (f32[512,512]{1,0:T(8,128)S(1)}, f32[512,512]{1,0:T(8,128)}, u32[]{:S(2)}) copy-start(f32[512,512]{1,0:T(8,128)} %copy-done.2) | copy-start | bytes 3145732

commit v2 on v1

--- a/solution.py
+++ b/solution.py
@@ -1,3 +1,5 @@
+import functools
+
 import jax
 import jax.numpy as jnp
 from jax import lax
@@ -5,18 +7,183 @@
 from jax.experimental.pallas import tpu as pltpu
 from jax.sharding import Mesh, PartitionSpec as P
 
-POWER = 2
 LANES = 128
 BLOCKS = [(r, c) for r in range(4) for c in range(r + 1)]
-
-
-def matmul(left, right):
-    return jnp.dot(left, right, precision=lax.Precision.HIGHEST, preferred_element_type=jnp.float32)
-
-
-def orthonormal(image):
-    small = jnp.linalg.cholesky(matmul(image.T, image))
-    return jax.scipy.linalg.solve_triangular(small, image.T, lower=True).T
+HIGHEST = lax.Precision.HIGHEST
+
+
+def three(x):
+    high = x.astype(jnp.bfloat16)
+    rest = x - high.astype(jnp.float32)
+    mid = rest.astype(jnp.bfloat16)
+    low = (rest - mid.astype(jnp.float32)).astype(jnp.bfloat16)
+    return high, mid, low
+
+
+def stack(x):
+    h, m, l = three(x)
+    return jnp.concatenate([h, h, m, h, l, m], 0), jnp.concatenate([h, m, h, l, h, m], 0)
+
+
+def dot_tn(left, right):
+    return lax.dot_general(left, right, (((0,), (0,)), ((), ())), preferred_element_type=jnp.float32)
+
+
+def lane(x, index):
+    return jnp.take_along_axis(x, index, axis=1)
+
+
+def row(x, k):
+    return jnp.broadcast_to(x[k : k + 1, :], (8, LANES))
+
+
+def eliminate(diag, groups, base):
+    nv = len(groups[0])
+    diag, groups = list(diag), [list(g) for g in groups]
+    zero = jnp.zeros((8, LANES), jnp.int32) + base
+    done = []
+    for j in range(4):
+        cols = {i: [lane(diag[i], zero + (8 * j + k)) for k in range(8)] for i in range(j, 4)}
+        a = {(m, k): row(cols[j][k], m) for k in range(8) for m in range(k, 8)}
+        scale, rows, drows = [], [], []
+        for k in range(8):
+            r = lax.rsqrt(a[k, k])
+            scale.append(r)
+            low = {m: a[m, k] * r for m in range(k + 1, 8)}
+            for m in range(k + 1, 8):
+                for q in range(k + 1, m + 1):
+                    a[m, q] = a[m, q] - low[m] * low[q]
+                a[m, k] = low[m]
+        for i in range(j + 1, 4):
+            for k in range(8):
+                c = cols[i][k]
+                for m in range(k):
+                    c = c - cols[i][m] * a[k, m]
+                cols[i][k] = c * scale[k]
+        for k in range(8):
+            d = row(diag[j], k)
+            g = [row(groups[j][v], k) for v in range(nv)]
+            for m in range(k):
+                d = d - a[k, m] * drows[m]
+                g = [g[v] - a[k, m] * rows[m][v] for v in range(nv)]
+            drows.append(d * scale[k])
+            rows.append([x * scale[k] for x in g])
+        for i in range(j + 1, 4):
+            for k in range(8):
+                diag[i] = diag[i] - cols[i][k] * drows[k]
+                groups[i] = [groups[i][v] - cols[i][k] * rows[k][v] for v in range(nv)]
+        done += rows
+    return done
+
+
+def chain_kernel(g_ref, x_ref, f_ref, fac_ref, basis_ref, core_ref, w, a_full, u, aug, ub, us, ubs, left, right):
+    inv = 1.0 / 262144
+    for i, (r, c) in enumerate(BLOCKS):
+        block = g_ref[i * LANES : (i + 1) * LANES, :] * inv
+        rs, cs = slice(r * LANES, (r + 1) * LANES), slice(c * LANES, (c + 1) * LANES)
+        w[rs, cs] = block
+        a_full[rs, cs] = block
+        if r != c:
+            flipped = block.T
+            w[cs, rs] = flipped
+            a_full[cs, rs] = flipped
+    left[...] = jnp.zeros_like(left)
+    right[...] = jnp.zeros_like(right)
+    aug[:, LANES:] = x_ref[...].T
+
+    def factor_step(s):
+        block = s // 4
+        base = lax.rem(s, 4) * 32
+        start = pl.multiple_of(s * 32, 32)
+        col = pl.multiple_of(block * LANES, LANES)
+        diag = [w[pl.ds(start + 8 * i, 8), pl.ds(col, LANES)] for i in range(4)]
+        groups = [[w[pl.ds(start + 8 * i, 8), v * LANES : (v + 1) * LANES] for v in range(4)] for i in range(4)]
+        lft, rgt = left, right
+        for q in range(1, 4):
+            other = pl.multiple_of(lax.rem(block + q, 4) * LANES, LANES)
+            w[pl.ds(other, LANES), :] -= dot_tn(lft[:, pl.ds(other, LANES)], rgt[...])
+        rows = eliminate(diag, groups, base)
+        for k in range(32):
+            for v in range(4):
+                us[k : k + 1, v * LANES : (v + 1) * LANES] = rows[k][v][0:1]
+        u[pl.ds(start, 32), :] = us[...]
+        lf, rg = stack(us[...])
+        left[...] = lf
+        right[...] = rg
+        nxt = pl.multiple_of(jnp.minimum((s + 1) // 4, 3) * LANES, LANES)
+        w[pl.ds(nxt, LANES), :] -= dot_tn(left[:, pl.ds(nxt, LANES)], rg)
+
+    def basis_step(q):
+        start = pl.multiple_of(q * 32, 32)
+        groups = [[aug[pl.ds(start + 8 * i, 8), v * LANES : (v + 1) * LANES] for v in range(5)] for i in range(4)]
+        rows = eliminate([g[0] for g in groups], groups, q * 32)
+        for k in range(32):
+            for v in range(5):
+                ubs[k : k + 1, v * LANES : (v + 1) * LANES] = rows[k][v][0:1]
+        ub[pl.ds(start, 32), :] = ubs[...]
+        lf, rg = stack(ubs[...])
+        aug[...] -= dot_tn(lf[:, :LANES], rg)
+
+    def power(t, carry):
+        @pl.when(t > 0)
+        def _():
+            aug[:, LANES:] = ub[:, LANES:]
+        image = jnp.dot(aug[:, LANES:], a_full[...], precision=HIGHEST, preferred_element_type=jnp.float32)
+        aug[:, LANES:] = image
+        aug[:, :LANES] = lax.dot_general(image, image, (((1,), (1,)), ((), ())), precision=HIGHEST, preferred_element_type=jnp.float32)
+
+        def both(q, c):
+            factor_step(4 * t + q)
+            basis_step(q)
+            return c
+        return lax.fori_loop(0, 4, both, carry)
+
+    lax.fori_loop(0, 2, power, 0)
+    basis_t = ub[:, LANES:]
+    basis_ref[...] = basis_t.T
+    fh = f_ref[...].astype(jnp.bfloat16)
+    fl = (f_ref[...] - fh.astype(jnp.float32)).astype(jnp.bfloat16)
+    bh = basis_t.astype(jnp.bfloat16)
+    bl = (basis_t - bh.astype(jnp.float32)).astype(jnp.bfloat16)
+    dot = functools.partial(jnp.dot, preferred_element_type=jnp.float32)
+    core = dot(bh, fh) + dot(bh, fl) + dot(bl, fh)
+    for c in range(4):
+        core_ref[pl.ds(c, LANES, stride=4), :] = core[:, c * LANES : (c + 1) * LANES]
+
+    def rest(s, c):
+        factor_step(s)
+        return c
+    lax.fori_loop(8, 16, rest, 0)
+    for r in range(4):
+        for c in range(4):
+            rs, cs = slice(r * LANES, (r + 1) * LANES), slice(c * LANES, (c + 1) * LANES)
+            if r < c:
+                fac_ref[rs, cs] = jnp.zeros((LANES, LANES), jnp.float32)
+            else:
+                block = u[cs, rs]
+                if r == c:
+                    up = lax.broadcasted_iota(jnp.int32, (LANES, LANES), 0) <= lax.broadcasted_iota(jnp.int32, (LANES, LANES), 1)
+                    block = jnp.where(up, block, 0.0)
+                fac_ref[rs, cs] = block.T
+
+
+def chain(packed, start_basis, flat):
+    f32, b16 = jnp.float32, jnp.bfloat16
+    return pl.pallas_call(
+        chain_kernel,
+        out_shape=(
+            jax.ShapeDtypeStruct((512, 512), f32),
+            jax.ShapeDtypeStruct((512, 128), f32),
+            jax.ShapeDtypeStruct((512, 128), f32),
+        ),
+        scratch_shapes=[
+            pltpu.VMEM((512, 512), f32), pltpu.VMEM((512, 512), f32), pltpu.VMEM((512, 512), f32),
+            pltpu.VMEM((128, 640), f32), pltpu.VMEM((128, 640), f32),
+            pltpu.VMEM((32, 512), f32), pltpu.VMEM((32, 640), f32),
+            pltpu.VMEM((192, 512), b16), pltpu.VMEM((192, 512), b16),
+        ],
+        compiler_params=pltpu.CompilerParams(vmem_limit_bytes=48 * 2**20),
+    )(packed, start_basis, flat)
 
 
 def split_kernel(x_ref, o_ref):
@@ -68,21 +235,11 @@
     return own.reshape(rows, LANES)
 
 
-def unpack(packed):
-    blocks = {b: packed[i * LANES : (i + 1) * LANES] for i, b in enumerate(BLOCKS)}
-    return jnp.block([[blocks[(r, c)] if r >= c else blocks[(c, r)].T for c in range(4)] for r in range(4)])
-
-
 def per_device(tensor, start_basis):
     regrouped = lax.all_to_all(split_columns(tensor), "mode", 0, 0, tiled=True)
     flat = regrouped.reshape(512, 512)
-    scaled = unpack(total_sum(packed_gram(flat))) / 262144
-    factor = jnp.linalg.cholesky(scaled)
-    basis = start_basis
-    for step in range(POWER):
-        basis = orthonormal(matmul(scaled, basis))
-    core = matmul(basis.T, flat).reshape(128, 1, 512)
-    return (factor, basis, core)
+    factor, basis, core = chain(total_sum(packed_gram(flat)), start_basis, flat)
+    return (factor, basis, core.reshape(128, 1, 512))
 
 
 def solution(mesh):

time: 253 us -> 131 us (0.52)
  other arithmetic: 127 us -> 0.08 us
  Pallas kernels: 6.22 us -> 29.7 us
  matrix products: 8.2 us -> 0 us
  local copies, waits for them, and re-layouts: 5.46 us -> 0.11 us
  between operations: 3.84 us -> 0.66 us
    another operation x25 -> x0, other arithmetic: 125 us -> none  [the longest x15 79.5 us: per_device(): factor = jnp.linalg.cholesky(scaled)]
    pallas_call x0 -> x1, Pallas kernels: none -> 23.6 us  [chain(): pl.pallas_call(chain_kernel, out_shape=(jax.ShapeDtypeStruct((512, 512),...]
    dot_general x5 -> x0, matrix products: 5.5 us -> none  [matmul(): jnp.dot(left, right, precision=lax.Precision.HIGHEST, preferred_element_t...]
    unnamed x18 -> x4, local copies, waits for them, and re-layouts: 4.3 us -> 0.01 us
    another operation x8 -> x0, matrix products: 2.7 us -> none  [the longest x6 1.87 us: per_device(): factor = jnp.linalg.cholesky(scaled)]
where the time goes in v2:
time: 131 us; the launch traced here: 130 us
  blocking collectives  99.5 us (76%)
  Pallas kernels  29.7 us (23%)
    all_to_all x1, blocking collectives, per_device(): regrouped = lax.all_to_all(split_columns(tensor), 'mode', 0, 0, tiled=True)  26.1 us
    pallas_call x1, Pallas kernels, chain(): pl.pallas_call(chain_kernel, out_shape=(jax.ShapeDtypeStruct((512, 512),...  23.6 us
    all_to_all x1, blocking collectives, total_sum(): own = lax.all_to_all(own, 'z', 0, 0, tiled=True).sum(0)  22.6 us
    all_to_all x1, blocking collectives, total_sum(): lax.all_to_all(jnp.broadcast_to(own, (32, *own.shape)), ('mode', 'x'), 0,...  19.6 us
    all_to_all x1, blocking collectives, total_sum(): lax.all_to_all(packed.reshape(32, rows // 32, LANES), ('mode', 'x'), 0, 0...  17.2 us
    all_to_all x1, blocking collectives, total_sum(): lax.all_to_all(jnp.broadcast_to(own, (16, 3, LANES)), 'z', 0, 0, tiled=True)  14 us
    pallas_call x1, Pallas kernels, packed_gram(): pl.pallas_call(gram_kernel, out_shape=jax.ShapeDtypeStruct((len(BLOCKS) *...  3.38 us
    pallas_call x1, Pallas kernels, split_columns(): pl.pallas_call(split_kernel, out_shape=jax.ShapeDtypeStruct((8, 64, 512),...  2.8 us

profile of v2, /device:TPU:1, one launch (start us, length us, event | category | flops | bytes accessed | tf_op | source)
XLA Modules:
  0.0 130.1 jit_solution(1914208244880900099)
XLA Ops:
  0.6 2.8 %shard_map.49 = f32[8,64,512]{2,1,0:T(8,128)} custom-call(f32[2048,128]{1,0:T(8,128)} %bitcast.9), custom_call_target="tpu_custom_call" | custom-call | tf_op jit(solution)/shard_map/pallas_call | solution.py:197
  3.4 26.1 %all_to_all.25 = f32[8,64,512]{2,1,0:T(8,128)} all-to-all(f32[8,64,512]{2,1,0:T(8,128)} %shard_map.49), channel_id=1, replica_groups=mesh['mode'=8,'z'=16,'x'=4] {'mode'}, dimensions={0} | all-to-all | bytes 2097152 | tf_op jit(solution)/shard_map/all_to_all | solution.py:239
  29.6 3.4 %shard_map.50 = f32[1280,128]{1,0:T(8,128)} custom-call(f32[512,512]{1,0:T(8,128)} %bitcast.5), custom_call_target="tpu_custom_call" | custom-call | tf_op jit(solution)/shard_map/pallas_call | solution.py:221
  33.0 17.2 %all_to_all.26 = f32[32,40,128]{2,1,0:T(8,128)S(1)} all-to-all(f32[32,40,128]{2,1,0:T(8,128)} %bitcast.8), channel_id=1, replica_groups=mesh['mode'=8,'z'=16,'x'=4] {'mode','x'}, dimensions={0} | all-to-all | bytes 1310720 | tf_op jit(solution)/shard_map/all_to_all | solution.py:229
  50.2 0.1 reduce_sum.18
  50.2 22.6 %all_to_all.27 = f32[16,3,128]{2,1,0:T(4,128)S(1)} all-to-all(f32[16,3,128]{2,1,0:T(4,128)S(1)} %reshape.30), channel_id=1, replica_groups=mesh['mode'=8,'z'=16,'x'=4] {'z'}, dimensions={0} | all-to-all | bytes 49152 | tf_op jit(solution)/shard_map/all_to_all | solution.py:231
  72.9 14.0 %all_to_all.28 = f32[16,3,128]{2,1,0:T(4,128)S(1)} all-to-all(f32[16,3,128]{2,1,0:T(4,128)S(1)} %broadcast_in_dim.6), channel_id=1, replica_groups=mesh['mode'=8,'z'=16,'x'=4] {'z'}, dimensions={0} | all-to-all | bytes 49152 | tf_op jit(solution)/shard_map/all_to_all | solution.py:232
  86.9 0.0 copy-start
  87.0 0.0 copy-start.1
  87.0 19.6 %all_to_all.29 = f32[32,40,128]{2,1,0:T(8,128)S(1)} all-to-all(f32[32,40,128]{2,1,0:T(8,128)S(1)} %broadcast_in_dim.7), channel_id=1, replica_groups=mesh['mode'=8,'z'=16,'x'=4] {'mode','x'}, dimensions={0} | all-to-all | bytes 1310720 | tf_op jit(solution)/shard_map/all_to_all | solution.py:234
  106.5 0.0 copy-done
  106.6 0.0 copy-done.1
  106.6 23.6 %shard_map.51 = (f32[512,512]{1,0:T(8,128)}, f32[512,128]{1,0:T(8,128)}, f32[512,128]{1,0:T(8,128)}) custom-call(f32[1280,128]{1,0:T(8,128)S(1)} %bitcast.7, f32[512,128]{1,0:T(8,128)S(1)} %copy-done.1, f32[512,512]{1,0:T(8,128)S(1)} %bitcast.6), custom_call_target="tpu_custom_call" | custom-call | tf_op jit(solution)/shard_map/pallas_call | solution.py:172
  (7 shorter events, 0.1 us)
Async XLA Ops:
  86.9 19.6 %copy-start = (f32[8,64,512]{2,1,0:T(8,128)S(1)}, f32[8,64,512]{2,1,0:T(8,128)}, u32[]{:S(2)}) copy-start(f32[8,64,512]{2,1,0:T(8,128)} %all_to_all.25) | copy-start | bytes 3145732
  87.0 19.6 %copy-start.1 = (f32[512,128]{1,0:T(8,128)S(1)}, f32[512,128]{1,0:T(8,128)}, u32[]{:S(2)}) copy-start(f32[512,128]{1,0:T(8,128)} %x_ref.1) | copy-start | bytes 786436

commit v3 on v2

--- a/solution.py
+++ b/solution.py
@@ -9,6 +9,9 @@
 
 LANES = 128
 BLOCKS = [(r, c) for r in range(4) for c in range(r + 1)]
+HALF = len(BLOCKS) // 2
+NEAR = ("y", "z_low", "x")
+FAR = ("z_high",)
 HIGHEST = lax.Precision.HIGHEST
 
 
@@ -76,17 +79,21 @@
     return done
 
 
-def chain_kernel(g_ref, x_ref, f_ref, fac_ref, basis_ref, core_ref, w, a_full, u, aug, ub, us, ubs, left, right):
-    inv = 1.0 / 262144
-    for i, (r, c) in enumerate(BLOCKS):
-        block = g_ref[i * LANES : (i + 1) * LANES, :] * inv
-        rs, cs = slice(r * LANES, (r + 1) * LANES), slice(c * LANES, (c + 1) * LANES)
-        w[rs, cs] = block
-        a_full[rs, cs] = block
-        if r != c:
-            flipped = block.T
-            w[cs, rs] = flipped
-            a_full[cs, rs] = flipped
+def chain_kernel(mine_ref, other_ref, x_ref, f_ref, fac_ref, basis_ref, core_ref, w, a_full, u, aug, ub, us, ubs, left, right):
+    core = lax.axis_index("core")
+    for me in range(2):
+        @pl.when(core == me)
+        def _():
+            for i, (r, c) in enumerate(BLOCKS):
+                ref = mine_ref if i // HALF == me else other_ref
+                block = ref[i % HALF * LANES : (i % HALF + 1) * LANES, :] * (1.0 / 262144)
+                rs, cs = slice(r * LANES, (r + 1) * LANES), slice(c * LANES, (c + 1) * LANES)
+                w[rs, cs] = block
+                a_full[rs, cs] = block
+                if r != c:
+                    flipped = block.T
+                    w[cs, rs] = flipped
+                    a_full[cs, rs] = flipped
     left[...] = jnp.zeros_like(left)
     right[...] = jnp.zeros_like(right)
     aug[:, LANES:] = x_ref[...].T
@@ -167,7 +174,7 @@
                 fac_ref[rs, cs] = block.T
 
 
-def chain(packed, start_basis, flat):
+def chain(mine, other, start_basis, flat):
     f32, b16 = jnp.float32, jnp.bfloat16
     return pl.pallas_call(
         chain_kernel,
@@ -182,8 +189,8 @@
             pltpu.VMEM((32, 512), f32), pltpu.VMEM((32, 640), f32),
             pltpu.VMEM((192, 512), b16), pltpu.VMEM((192, 512), b16),
         ],
-        compiler_params=pltpu.CompilerParams(vmem_limit_bytes=48 * 2**20),
-    )(packed, start_basis, flat)
+        compiler_params=pltpu.CompilerParams(vmem_limit_bytes=24 * 2**20),
+    )(mine, other, start_basis, flat)
 
 
 def split_kernel(x_ref, o_ref):
@@ -197,6 +204,7 @@
     return pl.pallas_call(
         split_kernel,
         out_shape=jax.ShapeDtypeStruct((8, 64, 512), jnp.float32),
+        compiler_params=pltpu.CompilerParams(vmem_limit_bytes=8 * 2**20),
     )(flat)
 
 
@@ -204,48 +212,57 @@
     return lax.dot_general(left, right, (((1,), (1,)), ((), ())), preferred_element_type=jnp.float32)
 
 
-def gram_kernel(f_ref, o_ref):
+def gram_kernel(f_ref, keep_ref, send_ref):
     full = f_ref[...]
     high = full.astype(jnp.bfloat16)
     low = (full - high.astype(jnp.float32)).astype(jnp.bfloat16)
+    blocks = []
     for r in range(4):
         rows = slice(r * LANES, (r + 1) * LANES)
         n = (r + 1) * LANES
         part = dot_t(high[rows], high[:n]) + dot_t(high[rows], low[:n]) + dot_t(low[rows], high[:n])
-        for c in range(r + 1):
-            start = BLOCKS.index((r, c)) * LANES
-            o_ref[start : start + LANES, :] = part[:, c * LANES : (c + 1) * LANES]
+        blocks += [part[:, c * LANES : (c + 1) * LANES] for c in range(r + 1)]
+    core = lax.axis_index("core")
+    for me in range(2):
+        @pl.when(core == me)
+        def _():
+            for i, block in enumerate(blocks):
+                ref = keep_ref if i // HALF == me else send_ref
+                ref[i % HALF * LANES : (i % HALF + 1) * LANES, :] = block
 
 
 def packed_gram(flat):
+    half = jax.ShapeDtypeStruct((HALF * LANES, LANES), jnp.float32)
     return pl.pallas_call(
-        gram_kernel,
-        out_shape=jax.ShapeDtypeStruct((len(BLOCKS) * LANES, LANES), jnp.float32),
+        gram_kernel, out_shape=(half, half), compiler_params=pltpu.CompilerParams(vmem_limit_bytes=12 * 2**20)
     )(flat)
 
 
-def total_sum(packed):
-    rows = packed.shape[0]
-    own = lax.all_to_all(packed.reshape(32, rows // 32, LANES), ("mode", "x"), 0, 0, tiled=True).sum(0)
-    own = jnp.pad(own, ((0, 8), (0, 0))).reshape(16, 3, LANES)
-    own = lax.all_to_all(own, "z", 0, 0, tiled=True).sum(0)
-    own = lax.all_to_all(jnp.broadcast_to(own, (16, 3, LANES)), "z", 0, 0, tiled=True)
-    own = own.reshape(48, LANES)[: rows // 32]
-    own = lax.all_to_all(jnp.broadcast_to(own, (32, *own.shape)), ("mode", "x"), 0, 0, tiled=True)
-    return own.reshape(rows, LANES)
+def swap_cores(x):
+    return lax.ppermute(x, "core", [(0, 1), (1, 0)])
+
+
+def total_sum(keep, send):
+    own = (keep + swap_cores(send)).reshape(32, 5, 4, LANES)
+    own = lax.all_to_all(own, NEAR, 0, 0, tiled=True).sum(0)
+    own = lax.all_to_all(jnp.broadcast_to(own, (8, 5, 4, LANES)), FAR, 0, 0, tiled=True).sum(0)
+    own = lax.all_to_all(jnp.broadcast_to(own, (32, 5, 4, LANES)), NEAR, 0, 0, tiled=True)
+    mine = own.reshape(HALF * LANES, LANES)
+    return mine, swap_cores(mine)
 
 
 def per_device(tensor, start_basis):
-    regrouped = lax.all_to_all(split_columns(tensor), "mode", 0, 0, tiled=True)
+    regrouped = lax.all_to_all(split_columns(tensor), ("y", "core"), 0, 0, tiled=True)
     flat = regrouped.reshape(512, 512)
-    factor, basis, core = chain(total_sum(packed_gram(flat)), start_basis, flat)
+    factor, basis, core = chain(*total_sum(*packed_gram(flat)), start_basis, flat)
     return (factor, basis, core.reshape(128, 1, 512))
 
 
 def solution(mesh):
-    grid = Mesh(mesh.devices.reshape(8, 16, 4), ("mode", "z", "x"))
-    in_specs = (P("mode", ("z", "x"), None), P())
-    out_specs = (P(), P(), P(None, ("z", "x"), "mode"))
+    grid = Mesh(mesh.devices.reshape(4, 2, 8, 2, 4), ("y", "core", "z_high", "z_low", "x"))
+    mode, col = ("y", "core"), ("z_high", "z_low", "x")
+    in_specs = (P(mode, col, None), P())
+    out_specs = (P(), P(), P(None, col, mode))
     return jax.shard_map(
         per_device, mesh=grid, in_specs=in_specs, out_specs=out_specs, check_vma=False
     )

time: 131 us -> 114 us (0.87)
  blocking collectives: 99.5 us -> 74.2 us
  starting transfers between devices: 0 us -> 9.37 us
  Pallas kernels: 29.7 us -> 25.6 us
  waiting for transfers between devices: 0 us -> 2.47 us
    all_to_all x5 -> x4, blocking collectives: 99.5 us -> 74.2 us  [the longest x1 25.6 us: total_sum(): lax.all_to_all(jnp.broadcast_to(own, (8, 5, 4, LANES)), FAR, 0, 0, tiled=...]
    ppermute x0 -> x2, starting transfers between devices: none -> 9.37 us  [swap_cores(): return lax.ppermute(x, 'core', [(0, 1), (1, 0)])]
    ppermute x0 -> x2, waiting for transfers between devices: none -> 2.47 us  [swap_cores(): return lax.ppermute(x, 'core', [(0, 1), (1, 0)])]
    pallas_call x1, Pallas kernels: 2.8 us -> 0.61 us  [split_columns(): pl.pallas_call(split_kernel, out_shape=jax.ShapeDtypeStruct((8, 64, 512),...]
    pallas_call x1, Pallas kernels: 3.38 us -> 1.35 us  [packed_gram(): pl.pallas_call(gram_kernel, out_shape=(half, half), compiler_params=pltpu...]
  transfers between devices with their start and end apart: 0 -> 2, of which waited for: 0 -> 2; matrix products, arithmetic and copies ran while one was open for 0% -> 0% of each run, Pallas kernels for 0% -> 0%
where the time goes in v3:
time: 114 us
  blocking collectives  74.2 us (65%)
  Pallas kernels  25.6 us (22%)
  starting transfers between devices  9.37 us (8%)
  waiting for transfers between devices  2.47 us (2%)
  local copies, waits for them, and re-layouts  1.28 us (1%)
    all_to_all x1, blocking collectives, total_sum(): lax.all_to_all(jnp.broadcast_to(own, (8, 5, 4, LANES)), FAR, 0, 0, tiled=...  25.6 us
    all_to_all x1, blocking collectives, per_device(): lax.all_to_all(split_columns(tensor), ('y', 'core'), 0, 0, tiled=True)  24.4 us
    pallas_call x1, Pallas kernels, chain(): pl.pallas_call(chain_kernel, out_shape=(jax.ShapeDtypeStruct((512, 512),...  23.6 us
    all_to_all x1, blocking collectives, total_sum(): lax.all_to_all(jnp.broadcast_to(own, (32, 5, 4, LANES)), NEAR, 0, 0, tile...  12.8 us
    all_to_all x1, blocking collectives, total_sum(): own = lax.all_to_all(own, NEAR, 0, 0, tiled=True).sum(0)  11.5 us
    ppermute x2, starting transfers between devices, swap_cores(): return lax.ppermute(x, 'core', [(0, 1), (1, 0)])  9.37 us
    ppermute x2, waiting for transfers between devices, swap_cores(): return lax.ppermute(x, 'core', [(0, 1), (1, 0)])  2.47 us
  transfers between devices with their start and end apart: 2, of which 2 were waited for; matrix products, arithmetic and copies ran while one was open for 0% of the time, Pallas kernels for 0%

profile of v3, /device:TPU:1, one launch (start us, length us, event | category | flops | bytes accessed | tf_op | source)
XLA Modules:
  0.0 113.8 jit_solution(7178736247846753572)
XLA Ops:
  0.6 0.0 copy-start
  0.6 1.2 %copy-done = f32[64,1,4096]{2,1,0:T(1,128)S(1)} copy-done((f32[64,1,4096]{2,1,0:T(1,128)S(1)}, f32[64,1,4096]{2,1,0:T(1,128)}, u32[]{:S(2)}) %copy-start) | copy-done | bytes 1048600
  1.9 0.6 shard_map.49
  2.5 24.4 %all_to_all.20 = f32[8,64,512]{2,1,0:T(8,128)S(1)} all-to-all(f32[8,64,512]{2,1,0:T(8,128)S(1)} %shard_map.49), channel_id=1, replica_groups=mesh['y'=4,'core'=2,'z_high'=8,'z_low'=2,'x'=4] {'y','core'}, dimensions={0} | all-to-all | bytes 2097152 | tf_op jit(solution)/shard_map/all_to_all | solution.py:255
  26.8 1.4 %shard_map.50 = (f32[640,128]{1,0:T(8,128)S(1)}, f32[640,128]{1,0:T(8,128)S(1)}) custom-call(f32[512,512]{1,0:T(8,128)S(1)} %bitcast.5), custom_call_target="tpu_custom_call" | custom-call | tf_op jit(solution)/shard_map/pallas_call | solution.py:236
  28.2 2.9 %collective-permute-start = (f32[640,128]{1,0:T(8,128)S(1)}, f32[640,128]{1,0:T(8,128)S(1)}, u32[]{:S(2)}, u32[]{:S(2)}) collective-permute-start(f32[640,128]{1,0:T(8,128)S(1)} %get-tuple-element.9), channel_id=1, source_target_pairs={{0,64},{64,0},{1,65},{65,1},{2,66},{66,2},{3,67},{67,3},{4,68},{68... | collective-permute-start | bytes 983048 | tf_op jit(solution)/shard_map/ppermute | solution.py:242
  31.1 1.2 %collective-permute-done = f32[640,128]{1,0:T(8,128)S(1)} collective-permute-done((f32[640,128]{1,0:T(8,128)S(1)}, f32[640,128]{1,0:T(8,128)S(1)}, u32[]{:S(2)}, u32[]{:S(2)}) %collective-permute-start) | collective-permute-done | bytes 327712 | tf_op jit(solution)/shard_map/ppermute | solution.py:242
  32.4 11.5 %all_to_all.21 = f32[32,5,4,128]{3,2,1,0:T(4,128)S(1)} all-to-all(f32[32,5,4,128]{3,2,1,0:T(4,128)S(1)} %bitcast.10), channel_id=1, replica_groups=mesh['y'=4,'core'=2,'z_high'=8,'z_low'=2,'x'=4] {'y','z_low','x'}, dimensions={0} | all-to-all | bytes 655360 | tf_op jit(solution)/shard_map/all_to_all | solution.py:247
  43.9 0.1 reduce_sum.18
  44.0 25.6 %all_to_all.22 = f32[8,5,4,128]{3,2,1,0:T(4,128)S(1)} all-to-all(f32[8,5,4,128]{3,2,1,0:T(4,128)S(1)} %broadcast_in_dim.6), channel_id=1, replica_groups=mesh['y'=4,'core'=2,'z_high'=8,'z_low'=2,'x'=4] {'z_high'}, dimensions={0} | all-to-all | bytes 163840 | tf_op jit(solution)/shard_map/all_to_all | solution.py:248
  69.6 0.0 copy-start.1
  69.6 12.8 %all_to_all.23 = f32[32,5,4,128]{3,2,1,0:T(4,128)S(1)} all-to-all(f32[32,5,4,128]{3,2,1,0:T(4,128)S(1)} %broadcast_in_dim.7), channel_id=1, replica_groups=mesh['y'=4,'core'=2,'z_high'=8,'z_low'=2,'x'=4] {'y','z_low','x'}, dimensions={0} | all-to-all | bytes 655360 | tf_op jit(solution)/shard_map/all_to_all | solution.py:249
  82.5 6.4 %collective-permute-start.1 = (f32[640,128]{1,0:T(8,128)S(1)}, f32[640,128]{1,0:T(8,128)S(1)}, u32[]{:S(2)}, u32[]{:S(2)}) collective-permute-start(f32[640,128]{1,0:T(8,128)S(1)} %bitcast.7), channel_id=1, source_target_pairs={{0,64},{64,0},{1,65},{65,1},{2,66},{66,2},{3,67},{67,3},{4,68},{68... | collective-permute-start | bytes 983048 | tf_op jit(solution)/shard_map/ppermute | solution.py:242
  88.9 1.2 %collective-permute-done.1.other_ref = f32[640,128]{1,0:T(8,128)S(1)} collective-permute-done((f32[640,128]{1,0:T(8,128)S(1)}, f32[640,128]{1,0:T(8,128)S(1)}, u32[]{:S(2)}, u32[]{:S(2)}) %collective-permute-start.1) | collective-permute-done | bytes 327712 | tf_op jit(solution)/shard_map/ppermute | solution.py:242
  90.1 0.0 copy-done.1
  90.1 23.6 %shard_map.51 = (f32[512,512]{1,0:T(8,128)}, f32[512,128]{1,0:T(8,128)}, f32[512,128]{1,0:T(8,128)}) custom-call(f32[640,128]{1,0:T(8,128)S(1)} %bitcast.8, f32[640,128]{1,0:T(8,128)S(1)} %collective-permute-done.1.other_ref, f32[512,128]{1,0:T(8,128)S(1)} %copy-done.1, f32[512,512]{1,0:T(8,128)S(1)} %bitcast.6), custom_call_target="tpu_custom_call" | custom-call | tf_op jit(solution)/shard_map/pallas_call | solution.py:179
  (4 shorter events, 0.1 us)
Async XLA Ops:
  0.6 1.2 %copy-start = (f32[64,1,4096]{2,1,0:T(1,128)S(1)}, f32[64,1,4096]{2,1,0:T(1,128)}, u32[]{:S(2)}) copy-start(f32[64,1,4096]{2,1,0:T(1,128)} %param.2) | copy-start | bytes 3145732
  28.2 4.2 %collective-permute-start = (f32[640,128]{1,0:T(8,128)S(1)}, f32[640,128]{1,0:T(8,128)S(1)}, u32[]{:S(2)}, u32[]{:S(2)}) collective-permute-start(f32[640,128]{1,0:T(8,128)S(1)} %get-tuple-element.9), channel_id=1, source_target_pairs={{0,64},{64,0},{1,65},{65,1},{2,66},{66,2},{3,67},{67,3},{4,68},{68... | collective-permute-start | bytes 983048 | tf_op jit(solution)/shard_map/ppermute | solution.py:242
  69.6 20.5 %copy-start.1 = (f32[512,128]{1,0:T(8,128)S(1)}, f32[512,128]{1,0:T(8,128)}, u32[]{:S(2)}) copy-start(f32[512,128]{1,0:T(8,128)} %x_ref.1) | copy-start | bytes 786436
  82.5 7.7 %collective-permute-start.1 = (f32[640,128]{1,0:T(8,128)S(1)}, f32[640,128]{1,0:T(8,128)S(1)}, u32[]{:S(2)}, u32[]{:S(2)}) collective-permute-start(f32[640,128]{1,0:T(8,128)S(1)} %bitcast.7), channel_id=1, source_target_pairs={{0,64},{64,0},{1,65},{65,1},{2,66},{66,2},{3,67},{67,3},{4,68},{68... | collective-permute-start | bytes 983048 | tf_op jit(solution)/shard_map/ppermute | solution.py:242

commit v4 on v3

v4 whole, which is shorter than its diff:
```python
import functools

import jax
import jax.numpy as jnp
from jax import lax
from jax.experimental import pallas as pl
from jax.experimental.pallas import tpu as pltpu
from jax.sharding import Mesh, PartitionSpec as P

LANES = 128
BLOCKS = [(r, c) for r in range(4) for c in range(r + 1)]
HALF = len(BLOCKS) // 2
NEAR = ("y", "z_low", "x")
FAR = ("z_high",)
PER_F, PER_B = 2, 1
HIGHEST = lax.Precision.HIGHEST


def three(x):
    high = x.astype(jnp.bfloat16)
    rest = x - high.astype(jnp.float32)
    mid = rest.astype(jnp.bfloat16)
    low = (rest - mid.astype(jnp.float32)).astype(jnp.bfloat16)
    return high, mid, low


def left_of(h, m, l):
    return jnp.concatenate([h, h, m, h, l, m], 0)


def right_of(h, m, l):
    return jnp.concatenate([h, m, h, l, h, m], 0)


def parts(ref):
    return [ref[i * 32 : i * 32 + 32, :] for i in range(3)]


def dot_tn(left, right):
    return lax.dot_general(left, right, (((0,), (0,)), ((), ())), preferred_element_type=jnp.float32)


def lane(x, index):
    return jnp.take_along_axis(x, index, axis=1)


def row(x, k):
    return jnp.broadcast_to(x[k : k + 1, :], (8, LANES))


def eliminate(diag, groups, base, packed, result, per):
    diag, groups = list(diag), [list(g) for g in groups]
    zero = jnp.zeros((8, LANES), jnp.int32) + base
    for j0 in range(0, 4, per):
        inside = range(j0, j0 + per)
        cols = {}
        for c in range(8 * per):
            for i in range(j0 + c // 8, 4):
                cols[i, c] = lane(diag[i], zero + (8 * j0 + c))
        for j in inside:
            for v in range(len(groups[j])):
                packed[64 * j + 8 * v : 64 * j + 8 * v + 8, :] = groups[j][v]
            packed[64 * j + 32 : 64 * j + 40, :] = diag[j]
        rows = {c: packed[pl.ds(64 * (j0 + c // 8) + c % 8, 8, stride=8), :] for c in range(8 * per)}
        for c in range(8 * per):
            own = j0 + c // 8
            r = lax.rsqrt(row(cols[own, c], c % 8))
            low = {}
            for c2 in range(c + 1, 8 * per):
                low[c2] = row(cols[j0 + c2 // 8, c], c2 % 8) * r
            for i in range(own, 4):
                cols[i, c] = cols[i, c] * r
            rows[c] = rows[c] * r
            for c2 in range(c + 1, 8 * per):
                for i in range(j0 + c2 // 8, 4):
                    cols[i, c2] = cols[i, c2] - cols[i, c] * low[c2]
                rows[c2] = rows[c2] - rows[c] * low[c2]
            result[pl.ds(64 * own + c % 8, 8, stride=8), :] = rows[c]
            if j0 + per < 4:
                for v in [4, *range(len(groups[0]))]:
                    u = row(rows[c], v)
                    for i in range(j0 + per, 4):
                        if v == 4:
                            diag[i] = diag[i] - cols[i, c] * u
                        else:
                            groups[i][v] = groups[i][v] - cols[i, c] * u
            yield


def run(*steps):
    steps = list(steps)
    while steps:
        steps = [s for s in steps if next(s, True) is None]


def gathered(result, blocks):
    return jnp.concatenate([jnp.concatenate([result[64 * j + 8 * v : 64 * j + 8 * v + 8, :] for j in range(4)], 0) for v in blocks], 1)


def chain_kernel(
    mine_ref, other_ref, x_ref, f_ref, fac_out, basis_out, core_out,
    w, a_high, a_low, u, aug, ub, packed_f, result_f, packed_b, result_b, split_f, split_b, turned_f, turned_b,
    fac, basis, core, sems,
):
    core_index = lax.axis_index("core")
    for me in range(2):
        @pl.when(core_index == me)
        def _():
            for i, (r, c) in enumerate(BLOCKS):
                ref = mine_ref if i // HALF == me else other_ref
                block = ref[i % HALF * LANES : (i % HALF + 1) * LANES, :] * (1.0 / 262144)
                for x, (p, q) in [(block, (r, c))] + ([(block.T, (c, r))] if r != c else []):
                    rs, cs = slice(p * LANES, (p + 1) * LANES), slice(q * LANES, (q + 1) * LANES)
                    w[rs, cs] = x
                    a_high[rs, cs], a_low[rs, cs] = two(x)
    zero_all = [packed_f, packed_b, split_f, u]
    for ref in zero_all:
        ref[...] = jnp.zeros_like(ref)
    w[512:, :] = jnp.zeros((32, 512), jnp.float32)
    aug[LANES:, :] = jnp.zeros((32, 640), jnp.float32)
    ub[:, LANES:] = x_ref[...].T

    def near_update(target, start, across, rows, turned):
        lf = left_of(*three(across)).T
        turned[...] = lf
        offset = pl.multiple_of(lax.rem(start, LANES), 32)
        target[pl.ds(start, 32), :] -= jnp.dot(turned[pl.ds(offset, 32), :], rows, preferred_element_type=jnp.float32)

    def factor_step(s):
        start = pl.multiple_of(s * 32, 32)
        col = pl.multiple_of(s // 4 * LANES, LANES)
        diag = [w[pl.ds(start + 8 * i, 8), pl.ds(col, LANES)] for i in range(4)]
        groups = [[w[pl.ds(start + 8 * i, 8), v * LANES : (v + 1) * LANES] for v in range(1, 4)] for i in range(4)]
        before = parts(split_f)
        lf, rg = left_of(*before), right_of(*before)
        for r in range(4):
            w[r * LANES : (r + 1) * LANES, r * LANES :] -= dot_tn(lf[:, r * LANES : (r + 1) * LANES], rg[:, r * LANES :])
        yield from eliminate(diag, groups, lax.rem(s, 4) * 32, packed_f, result_f, PER_F)
        u[pl.ds(start, 32), LANES:] = gathered(result_f, range(3))
        u[pl.ds(start, 32), pl.ds(col, LANES)] = gathered(result_f, [4])
        now = three(u[pl.ds(start, 32), :])
        split_f[...] = jnp.concatenate(now, 0)
        nxt = pl.multiple_of(jnp.minimum((s + 1) // 4, 3) * LANES, LANES)
        near_update(w, pl.multiple_of(start + 32, 32), u[pl.ds(start, 32), pl.ds(nxt, LANES)], right_of(*now), turned_f)

    def basis_step(q):
        start = pl.multiple_of(q * 32, 32)
        groups = [[aug[pl.ds(start + 8 * i, 8), v * LANES : (v + 1) * LANES] for v in range(5)] for i in range(4)]
        before = parts(split_b)
        aug[:LANES, :] -= dot_tn(left_of(*before)[:, :LANES], right_of(*before))
        yield from eliminate([g[0] for g in groups], [g[1:] for g in groups], q * 32, packed_b, result_b, PER_B)
        rows = gathered(result_b, [4, 0, 1, 2, 3])
        ub[pl.ds(start, 32), :] = rows
        now = three(rows)
        split_b[...] = jnp.concatenate(now, 0)
        near_update(aug, pl.multiple_of(start + 32, 32), rows[:, :LANES], right_of(*now), turned_b)

    def finish(r):
        rows = slice(r * LANES, (r + 1) * LANES)
        for c in range(4):
            cols = slice(c * LANES, (c + 1) * LANES)
            if c > r:
                fac[rows, cols] = jnp.zeros((LANES, LANES), jnp.float32)
                continue
            block = u[cols, rows].T
            if c == r:
                lower = lax.broadcasted_iota(jnp.int32, (LANES, LANES), 0) >= lax.broadcasted_iota(jnp.int32, (LANES, LANES), 1)
                block = jnp.where(lower, block, 0.0)
            fac[rows, cols] = block
        copy = pltpu.make_async_copy(fac.at[rows], fac_out.at[rows], sems.at[r])
        copy.start()
        return copy

    def image_step():
        high, low = two(ub[:, LANES:])
        image = dot(high, a_high[...]) + dot(high, a_low[...]) + dot(low, a_high[...])
        split_b[...] = jnp.zeros_like(split_b)
        aug[:LANES, LANES:] = image
        aug[:LANES, :LANES] = lax.dot_general(image, image, (((1,), (1,)), ((), ())), precision=HIGHEST, preferred_element_type=jnp.float32)

    def power(t, carry):
        image_step()
        run(factor_step(5 * t))

        def both(q, c):
            run(factor_step(5 * t + 1 + q), basis_step(q))
            return c
        return lax.fori_loop(0, 4, both, carry)

    lax.fori_loop(0, 2, power, 0)
    basis_t = ub[:, LANES:]
    basis[...] = basis_t.T
    copies = [pltpu.make_async_copy(basis, basis_out, sems.at[4])]
    copies[-1].start()
    bh, bl = two(basis_t)
    fh, fl = two(f_ref[...])
    product = dot(bh, fh) + dot(bh, fl) + dot(bl, fh)
    for c in range(4):
        core[pl.ds(c, LANES, stride=4), :] = product[:, c * LANES : (c + 1) * LANES]
    copies.append(pltpu.make_async_copy(core, core_out, sems.at[5]))
    copies[-1].start()
    run(factor_step(10))
    copies += [finish(0), finish(1)]

    def rest(s, c):
        run(factor_step(s))
        return c
    lax.fori_loop(11, 16, rest, 0)
    copies += [finish(2), finish(3)]
    for copy in copies:
        copy.wait()


def two(x):
    high = x.astype(jnp.bfloat16)
    return high, (x - high.astype(jnp.float32)).astype(jnp.bfloat16)


def dot(left, right):
    return jnp.dot(left, right, preferred_element_type=jnp.float32)


def chain(mine, other, start_basis, flat):
    f32, b16 = jnp.float32, jnp.bfloat16
    return pl.pallas_call(
        chain_kernel,
        out_shape=(
            jax.ShapeDtypeStruct((512, 512), f32),
            jax.ShapeDtypeStruct((512, 128), f32),
            jax.ShapeDtypeStruct((512, 128), f32),
        ),
        out_specs=[pl.BlockSpec(memory_space=pl.ANY)] * 3,
        scratch_shapes=[
            pltpu.VMEM((544, 512), f32), pltpu.VMEM((512, 512), b16), pltpu.VMEM((512, 512), b16), pltpu.VMEM((512, 512), f32),
            pltpu.VMEM((160, 640), f32), pltpu.VMEM((128, 640), f32),
            *[pltpu.VMEM((256, LANES), f32)] * 4,
            pltpu.VMEM((96, 512), b16), pltpu.VMEM((96, 640), b16),
            pltpu.VMEM((128, 192), b16), pltpu.VMEM((128, 192), b16),
            pltpu.VMEM((512, 512), f32), pltpu.VMEM((512, 128), f32), pltpu.VMEM((512, 128), f32),
            pltpu.SemaphoreType.DMA((6,)),
        ],
        compiler_params=pltpu.CompilerParams(vmem_limit_bytes=24 * 2**20),
    )(mine, other, start_basis, flat)


def split_kernel(x_ref, o_ref):
    for d in range(8):
        for c in range(4):
            o_ref[d, :, c * LANES : (c + 1) * LANES] = x_ref[pl.ds(d * 4 + c, 64, stride=32), :]


def split_columns(tensor):
    flat = tensor.reshape(64 * 32, LANES)
    return pl.pallas_call(
        split_kernel,
        out_shape=jax.ShapeDtypeStruct((8, 64, 512), jnp.float32),
        compiler_params=pltpu.CompilerParams(vmem_limit_bytes=8 * 2**20),
    )(flat)


def dot_t(left, right):
    return lax.dot_general(left, right, (((1,), (1,)), ((), ())), preferred_element_type=jnp.float32)


def gram_kernel(f_ref, keep_ref, send_ref):
    full = f_ref[...]
    high = full.astype(jnp.bfloat16)
    low = (full - high.astype(jnp.float32)).astype(jnp.bfloat16)
    blocks = []
    for r in range(4):
        rows = slice(r * LANES, (r + 1) * LANES)
        n = (r + 1) * LANES
        part = dot_t(high[rows], high[:n]) + dot_t(high[rows], low[:n]) + dot_t(low[rows], high[:n])
        blocks += [part[:, c * LANES : (c + 1) * LANES] for c in range(r + 1)]
    core = lax.axis_index("core")
    for me in range(2):
        @pl.when(core == me)
        def _():
            for i, block in enumerate(blocks):
                ref = keep_ref if i // HALF == me else send_ref
                ref[i % HALF * LANES : (i % HALF + 1) * LANES, :] = block


def packed_gram(flat):
    half = jax.ShapeDtypeStruct((HALF * LANES, LANES), jnp.float32)
    return pl.pallas_call(
        gram_kernel, out_shape=(half, half), compiler_params=pltpu.CompilerParams(vmem_limit_bytes=12 * 2**20)
    )(flat)


def swap_cores(x):
    return lax.ppermute(x, "core", [(0, 1), (1, 0)])


def total_sum(keep, send):
    own = (keep + swap_cores(send)).reshape(32, 5, 4, LANES)
    own = lax.all_to_all(own, NEAR, 0, 0, tiled=True).sum(0)
    own = lax.all_to_all(jnp.broadcast_to(own, (8, 5, 4, LANES)), FAR, 0, 0, tiled=True).sum(0)
    own = lax.all_to_all(jnp.broadcast_to(own, (32, 5, 4, LANES)), NEAR, 0, 0, tiled=True)
    mine = own.reshape(HALF * LANES, LANES)
    return mine, swap_cores(mine)


def per_device(tensor, start_basis):
    regrouped = lax.all_to_all(split_columns(tensor), ("y", "core"), 0, 0, tiled=True)
    flat = regrouped.reshape(512, 512)
    factor, basis, core = chain(*total_sum(*packed_gram(flat)), start_basis, flat)
    return (factor, basis, core.reshape(128, 1, 512))


def solution(mesh):
    grid = Mesh(mesh.devices.reshape(4, 2, 8, 2, 4), ("y", "core", "z_high", "z_low", "x"))
    mode, col = ("y", "core"), ("z_high", "z_low", "x")
    in_specs = (P(mode, col, None), P())
    out_specs = (P(), P(), P(None, col, mode))
    return jax.shard_map(
        per_device, mesh=grid, in_specs=in_specs, out_specs=out_specs, check_vma=False
    )
```

time: 114 us -> 108 us (0.947)
  Pallas kernels: 25.6 us -> 19.6 us
    pallas_call x1, Pallas kernels: 23.6 us -> 17.6 us  [chain(): pl.pallas_call(chain_kernel, out_shape=(jax.ShapeDtypeStruct((512, 512),...]
where the time goes in v4:
time: 108 us
  blocking collectives  74.2 us (69%)
  Pallas kernels  19.6 us (18%)
  starting transfers between devices  9.37 us (9%)
  waiting for transfers between devices  2.47 us (2%)
  local copies, waits for them, and re-layouts  1.28 us (1%)
    all_to_all x1, blocking collectives, total_sum(): lax.all_to_all(jnp.broadcast_to(own, (8, 5, 4, LANES)), FAR, 0, 0, tiled=...  25.6 us
    all_to_all x1, blocking collectives, per_device(): lax.all_to_all(split_columns(tensor), ('y', 'core'), 0, 0, tiled=True)  24.4 us
    pallas_call x1, Pallas kernels, chain(): pl.pallas_call(chain_kernel, out_shape=(jax.ShapeDtypeStruct((512, 512),...  17.6 us
    all_to_all x1, blocking collectives, total_sum(): lax.all_to_all(jnp.broadcast_to(own, (32, 5, 4, LANES)), NEAR, 0, 0, tile...  12.8 us
    all_to_all x1, blocking collectives, total_sum(): own = lax.all_to_all(own, NEAR, 0, 0, tiled=True).sum(0)  11.5 us
    ppermute x2, starting transfers between devices, swap_cores(): return lax.ppermute(x, 'core', [(0, 1), (1, 0)])  9.37 us
    ppermute x2, waiting for transfers between devices, swap_cores(): return lax.ppermute(x, 'core', [(0, 1), (1, 0)])  2.47 us
  transfers between devices with their start and end apart: 2, of which 2 were waited for; matrix products, arithmetic and copies ran while one was open for 0% of the time, Pallas kernels for 0%

profile of v4, /device:TPU:1, one launch (start us, length us, event | category | flops | bytes accessed | tf_op | source)
XLA Modules:
  0.0 107.8 jit_solution(2704117812654581574)
XLA Ops:
  0.6 0.0 copy-start
  0.6 1.2 %copy-done = f32[64,1,4096]{2,1,0:T(1,128)S(1)} copy-done((f32[64,1,4096]{2,1,0:T(1,128)S(1)}, f32[64,1,4096]{2,1,0:T(1,128)}, u32[]{:S(2)}) %copy-start) | copy-done | bytes 1048600
  1.9 0.6 shard_map.49
  2.5 24.4 %all_to_all.20 = f32[8,64,512]{2,1,0:T(8,128)S(1)} all-to-all(f32[8,64,512]{2,1,0:T(8,128)S(1)} %shard_map.49), channel_id=1, replica_groups=mesh['y'=4,'core'=2,'z_high'=8,'z_low'=2,'x'=4] {'y','core'}, dimensions={0} | all-to-all | bytes 2097152 | tf_op jit(solution)/shard_map/all_to_all | solution.py:305
  26.8 1.4 %shard_map.50 = (f32[640,128]{1,0:T(8,128)S(1)}, f32[640,128]{1,0:T(8,128)S(1)}) custom-call(f32[512,512]{1,0:T(8,128)S(1)} %bitcast.5), custom_call_target="tpu_custom_call" | custom-call | tf_op jit(solution)/shard_map/pallas_call | solution.py:286
  28.2 2.9 %collective-permute-start = (f32[640,128]{1,0:T(8,128)S(1)}, f32[640,128]{1,0:T(8,128)S(1)}, u32[]{:S(2)}, u32[]{:S(2)}) collective-permute-start(f32[640,128]{1,0:T(8,128)S(1)} %get-tuple-element.9), channel_id=1, source_target_pairs={{0,64},{64,0},{1,65},{65,1},{2,66},{66,2},{3,67},{67,3},{4,68},{68... | collective-permute-start | bytes 983048 | tf_op jit(solution)/shard_map/ppermute | solution.py:292
  31.1 1.2 %collective-permute-done = f32[640,128]{1,0:T(8,128)S(1)} collective-permute-done((f32[640,128]{1,0:T(8,128)S(1)}, f32[640,128]{1,0:T(8,128)S(1)}, u32[]{:S(2)}, u32[]{:S(2)}) %collective-permute-start) | collective-permute-done | bytes 327712 | tf_op jit(solution)/shard_map/ppermute | solution.py:292
  32.4 11.5 %all_to_all.21 = f32[32,5,4,128]{3,2,1,0:T(4,128)S(1)} all-to-all(f32[32,5,4,128]{3,2,1,0:T(4,128)S(1)} %bitcast.10), channel_id=1, replica_groups=mesh['y'=4,'core'=2,'z_high'=8,'z_low'=2,'x'=4] {'y','z_low','x'}, dimensions={0} | all-to-all | bytes 655360 | tf_op jit(solution)/shard_map/all_to_all | solution.py:297
  43.9 0.1 reduce_sum.18
  44.0 25.6 %all_to_all.22 = f32[8,5,4,128]{3,2,1,0:T(4,128)S(1)} all-to-all(f32[8,5,4,128]{3,2,1,0:T(4,128)S(1)} %broadcast_in_dim.6), channel_id=1, replica_groups=mesh['y'=4,'core'=2,'z_high'=8,'z_low'=2,'x'=4] {'z_high'}, dimensions={0} | all-to-all | bytes 163840 | tf_op jit(solution)/shard_map/all_to_all | solution.py:298
  69.6 0.0 copy-start.1
  69.6 12.8 %all_to_all.23 = f32[32,5,4,128]{3,2,1,0:T(4,128)S(1)} all-to-all(f32[32,5,4,128]{3,2,1,0:T(4,128)S(1)} %broadcast_in_dim.7), channel_id=1, replica_groups=mesh['y'=4,'core'=2,'z_high'=8,'z_low'=2,'x'=4] {'y','z_low','x'}, dimensions={0} | all-to-all | bytes 655360 | tf_op jit(solution)/shard_map/all_to_all | solution.py:299
  82.5 6.4 %collective-permute-start.1 = (f32[640,128]{1,0:T(8,128)S(1)}, f32[640,128]{1,0:T(8,128)S(1)}, u32[]{:S(2)}, u32[]{:S(2)}) collective-permute-start(f32[640,128]{1,0:T(8,128)S(1)} %bitcast.7), channel_id=1, source_target_pairs={{0,64},{64,0},{1,65},{65,1},{2,66},{66,2},{3,67},{67,3},{4,68},{68... | collective-permute-start | bytes 983048 | tf_op jit(solution)/shard_map/ppermute | solution.py:292
  88.9 1.2 %collective-permute-done.1.other_ref = f32[640,128]{1,0:T(8,128)S(1)} collective-permute-done((f32[640,128]{1,0:T(8,128)S(1)}, f32[640,128]{1,0:T(8,128)S(1)}, u32[]{:S(2)}, u32[]{:S(2)}) %collective-permute-start.1) | collective-permute-done | bytes 327712 | tf_op jit(solution)/shard_map/ppermute | solution.py:292
  90.1 0.0 copy-done.1
  90.1 17.6 %shard_map.51 = (f32[512,512]{1,0:T(8,128)}, f32[512,128]{1,0:T(8,128)}, f32[512,128]{1,0:T(8,128)}) custom-call(f32[640,128]{1,0:T(8,128)S(1)} %bitcast.8, f32[640,128]{1,0:T(8,128)S(1)} %collective-permute-done.1.other_ref, f32[512,128]{1,0:T(8,128)S(1)} %copy-done.1, f32[512,512]{1,0:T(8,128)S(1)} %bitcast.6), custom_call_target="tpu_custom_call" | custom-call | tf_op jit(solution)/shard_map/pallas_call | solution.py:225
  (4 shorter events, 0.1 us)
Async XLA Ops:
  0.6 1.2 %copy-start = (f32[64,1,4096]{2,1,0:T(1,128)S(1)}, f32[64,1,4096]{2,1,0:T(1,128)}, u32[]{:S(2)}) copy-start(f32[64,1,4096]{2,1,0:T(1,128)} %param.2) | copy-start | bytes 3145732
  28.2 4.2 %collective-permute-start = (f32[640,128]{1,0:T(8,128)S(1)}, f32[640,128]{1,0:T(8,128)S(1)}, u32[]{:S(2)}, u32[]{:S(2)}) collective-permute-start(f32[640,128]{1,0:T(8,128)S(1)} %get-tuple-element.9), channel_id=1, source_target_pairs={{0,64},{64,0},{1,65},{65,1},{2,66},{66,2},{3,67},{67,3},{4,68},{68... | collective-permute-start | bytes 983048 | tf_op jit(solution)/shard_map/ppermute | solution.py:292
  69.6 20.5 %copy-start.1 = (f32[512,128]{1,0:T(8,128)S(1)}, f32[512,128]{1,0:T(8,128)}, u32[]{:S(2)}) copy-start(f32[512,128]{1,0:T(8,128)} %x_ref.1) | copy-start | bytes 786436
  82.5 7.7 %collective-permute-start.1 = (f32[640,128]{1,0:T(8,128)S(1)}, f32[640,128]{1,0:T(8,128)S(1)}, u32[]{:S(2)}, u32[]{:S(2)}) collective-permute-start(f32[640,128]{1,0:T(8,128)S(1)} %bitcast.7), channel_id=1, source_target_pairs={{0,64},{64,0},{1,65},{65,1},{2,66},{66,2},{3,67},{67,3},{4,68},{68... | collective-permute-start | bytes 983048 | tf_op jit(solution)/shard_map/ppermute | solution.py:292

commit v5 on v4

--- a/solution.py
+++ b/solution.py
@@ -12,28 +12,19 @@
 HALF = len(BLOCKS) // 2
 NEAR = ("y", "z_low", "x")
 FAR = ("z_high",)
-PER_F, PER_B = 2, 1
-HIGHEST = lax.Precision.HIGHEST
-
-
-def three(x):
-    high = x.astype(jnp.bfloat16)
-    rest = x - high.astype(jnp.float32)
-    mid = rest.astype(jnp.bfloat16)
-    low = (rest - mid.astype(jnp.float32)).astype(jnp.bfloat16)
-    return high, mid, low
-
-
-def left_of(h, m, l):
-    return jnp.concatenate([h, h, m, h, l, m], 0)
-
-
-def right_of(h, m, l):
-    return jnp.concatenate([h, m, h, l, h, m], 0)
+PER_F, PER_B = (2, 2, 2, 2), 1
+
+
+def left_of(h, l):
+    return jnp.concatenate([h, h, l], 0)
+
+
+def right_of(h, l):
+    return jnp.concatenate([h, l, h], 0)
 
 
 def parts(ref):
-    return [ref[i * 32 : i * 32 + 32, :] for i in range(3)]
+    return [ref[i * 32 : i * 32 + 32, :] for i in range(2)]
 
 
 def dot_tn(left, right):
@@ -120,28 +111,29 @@
     aug[LANES:, :] = jnp.zeros((32, 640), jnp.float32)
     ub[:, LANES:] = x_ref[...].T
 
-    def near_update(target, start, across, rows, turned):
-        lf = left_of(*three(across)).T
+    def near_update(target, start, across, rows, turned, first):
+        lf = left_of(*two(across)).T
         turned[...] = lf
         offset = pl.multiple_of(lax.rem(start, LANES), 32)
-        target[pl.ds(start, 32), :] -= jnp.dot(turned[pl.ds(offset, 32), :], rows, preferred_element_type=jnp.float32)
-
-    def factor_step(s):
+        target[pl.ds(start, 32), first * LANES :] -= jnp.dot(turned[pl.ds(offset, 32), :], rows, preferred_element_type=jnp.float32)
+
+    def factor_step(s, first):
         start = pl.multiple_of(s * 32, 32)
         col = pl.multiple_of(s // 4 * LANES, LANES)
         diag = [w[pl.ds(start + 8 * i, 8), pl.ds(col, LANES)] for i in range(4)]
-        groups = [[w[pl.ds(start + 8 * i, 8), v * LANES : (v + 1) * LANES] for v in range(1, 4)] for i in range(4)]
+        groups = [[w[pl.ds(start + 8 * i, 8), v * LANES : (v + 1) * LANES] for v in range(first + 1, 4)] for i in range(4)]
         before = parts(split_f)
         lf, rg = left_of(*before), right_of(*before)
-        for r in range(4):
+        for r in range(first, 4):
             w[r * LANES : (r + 1) * LANES, r * LANES :] -= dot_tn(lf[:, r * LANES : (r + 1) * LANES], rg[:, r * LANES :])
-        yield from eliminate(diag, groups, lax.rem(s, 4) * 32, packed_f, result_f, PER_F)
-        u[pl.ds(start, 32), LANES:] = gathered(result_f, range(3))
+        yield from eliminate(diag, groups, lax.rem(s, 4) * 32, packed_f, result_f, PER_F[first])
+        if first < 3:
+            u[pl.ds(start, 32), (first + 1) * LANES :] = gathered(result_f, range(3 - first))
         u[pl.ds(start, 32), pl.ds(col, LANES)] = gathered(result_f, [4])
-        now = three(u[pl.ds(start, 32), :])
-        split_f[...] = jnp.concatenate(now, 0)
+        now = two(u[pl.ds(start, 32), first * LANES :])
+        split_f[:, first * LANES :] = jnp.concatenate(now, 0)
         nxt = pl.multiple_of(jnp.minimum((s + 1) // 4, 3) * LANES, LANES)
-        near_update(w, pl.multiple_of(start + 32, 32), u[pl.ds(start, 32), pl.ds(nxt, LANES)], right_of(*now), turned_f)
+        near_update(w, pl.multiple_of(start + 32, 32), u[pl.ds(start, 32), pl.ds(nxt, LANES)], right_of(*now), turned_f, first)
 
     def basis_step(q):
         start = pl.multiple_of(q * 32, 32)
@@ -151,13 +143,13 @@
         yield from eliminate([g[0] for g in groups], [g[1:] for g in groups], q * 32, packed_b, result_b, PER_B)
         rows = gathered(result_b, [4, 0, 1, 2, 3])
         ub[pl.ds(start, 32), :] = rows
-        now = three(rows)
+        now = two(rows)
         split_b[...] = jnp.concatenate(now, 0)
-        near_update(aug, pl.multiple_of(start + 32, 32), rows[:, :LANES], right_of(*now), turned_b)
-
-    def finish(r):
+        near_update(aug, pl.multiple_of(start + 32, 32), rows[:, :LANES], right_of(*now), turned_b, 0)
+
+    def finish(r, first, last, sem):
         rows = slice(r * LANES, (r + 1) * LANES)
-        for c in range(4):
+        for c in range(first, last):
             cols = slice(c * LANES, (c + 1) * LANES)
             if c > r:
                 fac[rows, cols] = jnp.zeros((LANES, LANES), jnp.float32)
@@ -167,7 +159,8 @@
                 lower = lax.broadcasted_iota(jnp.int32, (LANES, LANES), 0) >= lax.broadcasted_iota(jnp.int32, (LANES, LANES), 1)
                 block = jnp.where(lower, block, 0.0)
             fac[rows, cols] = block
-        copy = pltpu.make_async_copy(fac.at[rows], fac_out.at[rows], sems.at[r])
+        cols = slice(first * LANES, last * LANES)
+        copy = pltpu.make_async_copy(fac.at[rows, cols], fac_out.at[rows, cols], sems.at[sem])
         copy.start()
         return copy
 
@@ -176,18 +169,19 @@
         image = dot(high, a_high[...]) + dot(high, a_low[...]) + dot(low, a_high[...])
         split_b[...] = jnp.zeros_like(split_b)
         aug[:LANES, LANES:] = image
-        aug[:LANES, :LANES] = lax.dot_general(image, image, (((1,), (1,)), ((), ())), precision=HIGHEST, preferred_element_type=jnp.float32)
-
-    def power(t, carry):
+        high, low = two(image)
+        cross = dot_nt(high, low)
+        aug[:LANES, :LANES] = dot_nt(high, high) + cross + cross.T
+
+    for t in range(2):
         image_step()
-        run(factor_step(5 * t))
+        run(factor_step(5 * t, t))
 
         def both(q, c):
-            run(factor_step(5 * t + 1 + q), basis_step(q))
+            run(basis_step(q), factor_step(5 * t + 1 + q, t))
             return c
-        return lax.fori_loop(0, 4, both, carry)
-
-    lax.fori_loop(0, 2, power, 0)
+        lax.fori_loop(0, 4, both, 0)
+
     basis_t = ub[:, LANES:]
     basis[...] = basis_t.T
     copies = [pltpu.make_async_copy(basis, basis_out, sems.at[4])]
@@ -199,14 +193,18 @@
         core[pl.ds(c, LANES, stride=4), :] = product[:, c * LANES : (c + 1) * LANES]
     copies.append(pltpu.make_async_copy(core, core_out, sems.at[5]))
     copies[-1].start()
-    run(factor_step(10))
-    copies += [finish(0), finish(1)]
+    run(factor_step(10, 2))
+    copies.append(finish(0, 0, 4, 0))
+    run(factor_step(11, 2))
+    copies.append(finish(1, 0, 4, 1))
 
     def rest(s, c):
-        run(factor_step(s))
+        run(factor_step(s, 3))
         return c
-    lax.fori_loop(11, 16, rest, 0)
-    copies += [finish(2), finish(3)]
+    run(factor_step(12, 3))
+    copies += [finish(2, 0, 4, 2), finish(3, 0, 3, 3)]
+    lax.fori_loop(13, 16, rest, 0)
+    copies.append(finish(3, 3, 4, 6))
     for copy in copies:
         copy.wait()
 
@@ -214,6 +212,10 @@
 def two(x):
     high = x.astype(jnp.bfloat16)
     return high, (x - high.astype(jnp.float32)).astype(jnp.bfloat16)
+
+
+def dot_nt(left, right):
+    return lax.dot_general(left, right, (((1,), (1,)), ((), ())), preferred_element_type=jnp.float32)
 
 
 def dot(left, right):
@@ -234,10 +236,10 @@
             pltpu.VMEM((544, 512), f32), pltpu.VMEM((512, 512), b16), pltpu.VMEM((512, 512), b16), pltpu.VMEM((512, 512), f32),
             pltpu.VMEM((160, 640), f32), pltpu.VMEM((128, 640), f32),
             *[pltpu.VMEM((256, LANES), f32)] * 4,
-            pltpu.VMEM((96, 512), b16), pltpu.VMEM((96, 640), b16),
-            pltpu.VMEM((128, 192), b16), pltpu.VMEM((128, 192), b16),
+            pltpu.VMEM((64, 512), b16), pltpu.VMEM((64, 640), b16),
+            pltpu.VMEM((128, 96), b16), pltpu.VMEM((128, 96), b16),
             pltpu.VMEM((512, 512), f32), pltpu.VMEM((512, 128), f32), pltpu.VMEM((512, 128), f32),
-            pltpu.SemaphoreType.DMA((6,)),
+            pltpu.SemaphoreType.DMA((7,)),
         ],
         compiler_params=pltpu.CompilerParams(vmem_limit_bytes=24 * 2**20),
     )(mine, other, start_basis, flat)

time: 108 us -> 106 us (0.981)
  Pallas kernels: 19.6 us -> 17.8 us
    pallas_call x1, Pallas kernels: 17.6 us -> 15.8 us  [chain(): pl.pallas_call(chain_kernel, out_shape=(jax.ShapeDtypeStruct((512, 512),...]
where the time goes in v5:
time: 106 us
  blocking collectives  74.2 us (70%)
  Pallas kernels  17.8 us (17%)
  starting transfers between devices  9.37 us (9%)
  waiting for transfers between devices  2.47 us (2%)
  local copies, waits for them, and re-layouts  1.28 us (1%)
    all_to_all x1, blocking collectives, total_sum(): lax.all_to_all(jnp.broadcast_to(own, (8, 5, 4, LANES)), FAR, 0, 0, tiled=...  25.6 us
    all_to_all x1, blocking collectives, per_device(): lax.all_to_all(split_columns(tensor), ('y', 'core'), 0, 0, tiled=True)  24.4 us
    pallas_call x1, Pallas kernels, chain(): pl.pallas_call(chain_kernel, out_shape=(jax.ShapeDtypeStruct((512, 512),...  15.8 us
    all_to_all x1, blocking collectives, total_sum(): lax.all_to_all(jnp.broadcast_to(own, (32, 5, 4, LANES)), NEAR, 0, 0, tile...  12.8 us
    all_to_all x1, blocking collectives, total_sum(): own = lax.all_to_all(own, NEAR, 0, 0, tiled=True).sum(0)  11.5 us
    ppermute x2, starting transfers between devices, swap_cores(): return lax.ppermute(x, 'core', [(0, 1), (1, 0)])  9.37 us
    ppermute x2, waiting for transfers between devices, swap_cores(): return lax.ppermute(x, 'core', [(0, 1), (1, 0)])  2.47 us
  transfers between devices with their start and end apart: 2, of which 2 were waited for; matrix products, arithmetic and copies ran while one was open for 0% of the time, Pallas kernels for 0%

profile of v5, /device:TPU:1, one launch (start us, length us, event | category | flops | bytes accessed | tf_op | source)
XLA Modules:
  0.0 106.0 jit_solution(6604535402903367338)
XLA Ops:
  0.6 0.0 copy-start
  0.6 1.2 %copy-done = f32[64,1,4096]{2,1,0:T(1,128)S(1)} copy-done((f32[64,1,4096]{2,1,0:T(1,128)S(1)}, f32[64,1,4096]{2,1,0:T(1,128)}, u32[]{:S(2)}) %copy-start) | copy-done | bytes 1048600
  1.9 0.6 shard_map.49
  2.5 24.4 %all_to_all.20 = f32[8,64,512]{2,1,0:T(8,128)S(1)} all-to-all(f32[8,64,512]{2,1,0:T(8,128)S(1)} %shard_map.49), channel_id=1, replica_groups=mesh['y'=4,'core'=2,'z_high'=8,'z_low'=2,'x'=4] {'y','core'}, dimensions={0} | all-to-all | bytes 2097152 | tf_op jit(solution)/shard_map/all_to_all | solution.py:307
  26.8 1.4 %shard_map.50 = (f32[640,128]{1,0:T(8,128)S(1)}, f32[640,128]{1,0:T(8,128)S(1)}) custom-call(f32[512,512]{1,0:T(8,128)S(1)} %bitcast.5), custom_call_target="tpu_custom_call" | custom-call | tf_op jit(solution)/shard_map/pallas_call | solution.py:288
  28.2 2.9 %collective-permute-start = (f32[640,128]{1,0:T(8,128)S(1)}, f32[640,128]{1,0:T(8,128)S(1)}, u32[]{:S(2)}, u32[]{:S(2)}) collective-permute-start(f32[640,128]{1,0:T(8,128)S(1)} %get-tuple-element.9), channel_id=1, source_target_pairs={{0,64},{64,0},{1,65},{65,1},{2,66},{66,2},{3,67},{67,3},{4,68},{68... | collective-permute-start | bytes 983048 | tf_op jit(solution)/shard_map/ppermute | solution.py:294
  31.1 1.2 %collective-permute-done = f32[640,128]{1,0:T(8,128)S(1)} collective-permute-done((f32[640,128]{1,0:T(8,128)S(1)}, f32[640,128]{1,0:T(8,128)S(1)}, u32[]{:S(2)}, u32[]{:S(2)}) %collective-permute-start) | collective-permute-done | bytes 327712 | tf_op jit(solution)/shard_map/ppermute | solution.py:294
  32.4 11.5 %all_to_all.21 = f32[32,5,4,128]{3,2,1,0:T(4,128)S(1)} all-to-all(f32[32,5,4,128]{3,2,1,0:T(4,128)S(1)} %bitcast.10), channel_id=1, replica_groups=mesh['y'=4,'core'=2,'z_high'=8,'z_low'=2,'x'=4] {'y','z_low','x'}, dimensions={0} | all-to-all | bytes 655360 | tf_op jit(solution)/shard_map/all_to_all | solution.py:299
  43.9 0.1 reduce_sum.18
  44.0 25.6 %all_to_all.22 = f32[8,5,4,128]{3,2,1,0:T(4,128)S(1)} all-to-all(f32[8,5,4,128]{3,2,1,0:T(4,128)S(1)} %broadcast_in_dim.6), channel_id=1, replica_groups=mesh['y'=4,'core'=2,'z_high'=8,'z_low'=2,'x'=4] {'z_high'}, dimensions={0} | all-to-all | bytes 163840 | tf_op jit(solution)/shard_map/all_to_all | solution.py:300
  69.6 0.0 copy-start.1
  69.6 12.8 %all_to_all.23 = f32[32,5,4,128]{3,2,1,0:T(4,128)S(1)} all-to-all(f32[32,5,4,128]{3,2,1,0:T(4,128)S(1)} %broadcast_in_dim.7), channel_id=1, replica_groups=mesh['y'=4,'core'=2,'z_high'=8,'z_low'=2,'x'=4] {'y','z_low','x'}, dimensions={0} | all-to-all | bytes 655360 | tf_op jit(solution)/shard_map/all_to_all | solution.py:301
  82.5 6.4 %collective-permute-start.1 = (f32[640,128]{1,0:T(8,128)S(1)}, f32[640,128]{1,0:T(8,128)S(1)}, u32[]{:S(2)}, u32[]{:S(2)}) collective-permute-start(f32[640,128]{1,0:T(8,128)S(1)} %bitcast.7), channel_id=1, source_target_pairs={{0,64},{64,0},{1,65},{65,1},{2,66},{66,2},{3,67},{67,3},{4,68},{68... | collective-permute-start | bytes 983048 | tf_op jit(solution)/shard_map/ppermute | solution.py:294
  88.9 1.2 %collective-permute-done.1.other_ref = f32[640,128]{1,0:T(8,128)S(1)} collective-permute-done((f32[640,128]{1,0:T(8,128)S(1)}, f32[640,128]{1,0:T(8,128)S(1)}, u32[]{:S(2)}, u32[]{:S(2)}) %collective-permute-start.1) | collective-permute-done | bytes 327712 | tf_op jit(solution)/shard_map/ppermute | solution.py:294
  90.1 0.0 copy-done.1
  90.1 15.8 %shard_map.51 = (f32[512,512]{1,0:T(8,128)}, f32[512,128]{1,0:T(8,128)}, f32[512,128]{1,0:T(8,128)}) custom-call(f32[640,128]{1,0:T(8,128)S(1)} %bitcast.8, f32[640,128]{1,0:T(8,128)S(1)} %collective-permute-done.1.other_ref, f32[512,128]{1,0:T(8,128)S(1)} %copy-done.1, f32[512,512]{1,0:T(8,128)S(1)} %bitcast.6), custom_call_target="tpu_custom_call" | custom-call | tf_op jit(solution)/shard_map/pallas_call | solution.py:227
  (4 shorter events, 0.1 us)
Async XLA Ops:
  0.6 1.2 %copy-start = (f32[64,1,4096]{2,1,0:T(1,128)S(1)}, f32[64,1,4096]{2,1,0:T(1,128)}, u32[]{:S(2)}) copy-start(f32[64,1,4096]{2,1,0:T(1,128)} %param.2) | copy-start | bytes 3145732
  28.2 4.2 %collective-permute-start = (f32[640,128]{1,0:T(8,128)S(1)}, f32[640,128]{1,0:T(8,128)S(1)}, u32[]{:S(2)}, u32[]{:S(2)}) collective-permute-start(f32[640,128]{1,0:T(8,128)S(1)} %get-tuple-element.9), channel_id=1, source_target_pairs={{0,64},{64,0},{1,65},{65,1},{2,66},{66,2},{3,67},{67,3},{4,68},{68... | collective-permute-start | bytes 983048 | tf_op jit(solution)/shard_map/ppermute | solution.py:294
  69.6 20.5 %copy-start.1 = (f32[512,128]{1,0:T(8,128)S(1)}, f32[512,128]{1,0:T(8,128)}, u32[]{:S(2)}) copy-start(f32[512,128]{1,0:T(8,128)} %x_ref.1) | copy-start | bytes 786436
  82.5 7.7 %collective-permute-start.1 = (f32[640,128]{1,0:T(8,128)S(1)}, f32[640,128]{1,0:T(8,128)S(1)}, u32[]{:S(2)}, u32[]{:S(2)}) collective-permute-start(f32[640,128]{1,0:T(8,128)S(1)} %bitcast.7), channel_id=1, source_target_pairs={{0,64},{64,0},{1,65},{65,1},{2,66},{66,2},{3,67},{67,3},{4,68},{68... | collective-permute-start | bytes 983048 | tf_op jit(solution)/shard_map/ppermute | solution.py:294

commit v6 on v5

--- a/solution.py
+++ b/solution.py
@@ -264,29 +264,34 @@
     return lax.dot_general(left, right, (((1,), (1,)), ((), ())), preferred_element_type=jnp.float32)
 
 
-def gram_kernel(f_ref, keep_ref, send_ref):
+def gram_kernel(f_ref, o_ref, *, kept):
     full = f_ref[...]
     high = full.astype(jnp.bfloat16)
     low = (full - high.astype(jnp.float32)).astype(jnp.bfloat16)
-    blocks = []
-    for r in range(4):
-        rows = slice(r * LANES, (r + 1) * LANES)
-        n = (r + 1) * LANES
-        part = dot_t(high[rows], high[:n]) + dot_t(high[rows], low[:n]) + dot_t(low[rows], high[:n])
-        blocks += [part[:, c * LANES : (c + 1) * LANES] for c in range(r + 1)]
     core = lax.axis_index("core")
-    for me in range(2):
-        @pl.when(core == me)
+    for half in range(2):
+        @pl.when((core == half) == kept)
         def _():
-            for i, block in enumerate(blocks):
-                ref = keep_ref if i // HALF == me else send_ref
-                ref[i % HALF * LANES : (i % HALF + 1) * LANES, :] = block
-
-
-def packed_gram(flat):
-    half = jax.ShapeDtypeStruct((HALF * LANES, LANES), jnp.float32)
+            blocks = BLOCKS[half * HALF : (half + 1) * HALF]
+            at = 0
+            for r in range(4):
+                across = [c for row_block, c in blocks if row_block == r]
+                if not across:
+                    continue
+                rows = slice(r * LANES, (r + 1) * LANES)
+                cols = slice(across[0] * LANES, (across[-1] + 1) * LANES)
+                part = dot_t(high[rows], high[cols]) + dot_t(high[rows], low[cols]) + dot_t(low[rows], high[cols])
+                for i in range(len(across)):
+                    o_ref[at : at + LANES, :] = part[:, i * LANES : (i + 1) * LANES]
+                    at += LANES
+
+
+def half_gram(flat, kept):
     return pl.pallas_call(
-        gram_kernel, out_shape=(half, half), compiler_params=pltpu.CompilerParams(vmem_limit_bytes=12 * 2**20)
+        functools.partial(gram_kernel, kept=kept),
+        out_shape=jax.ShapeDtypeStruct((HALF * LANES, LANES), jnp.float32),
+        compiler_params=pltpu.CompilerParams(vmem_limit_bytes=12 * 2**20),
+        cost_estimate=pl.CostEstimate(flops=6 * 5 * 128 * 128 * 512, bytes_accessed=1400000, transcendentals=0),
     )(flat)
 
 
@@ -294,8 +299,9 @@
     return lax.ppermute(x, "core", [(0, 1), (1, 0)])
 
 
-def total_sum(keep, send):
-    own = (keep + swap_cores(send)).reshape(32, 5, 4, LANES)
+def total_sum(flat):
+    came = swap_cores(half_gram(flat, False))
+    own = (half_gram(flat, True) + came).reshape(32, 5, 4, LANES)
     own = lax.all_to_all(own, NEAR, 0, 0, tiled=True).sum(0)
     own = lax.all_to_all(jnp.broadcast_to(own, (8, 5, 4, LANES)), FAR, 0, 0, tiled=True).sum(0)
     own = lax.all_to_all(jnp.broadcast_to(own, (32, 5, 4, LANES)), NEAR, 0, 0, tiled=True)
@@ -306,7 +312,7 @@
 def per_device(tensor, start_basis):
     regrouped = lax.all_to_all(split_columns(tensor), ("y", "core"), 0, 0, tiled=True)
     flat = regrouped.reshape(512, 512)
-    factor, basis, core = chain(*total_sum(*packed_gram(flat)), start_basis, flat)
+    factor, basis, core = chain(*total_sum(flat), start_basis, flat)
     return (factor, basis, core.reshape(128, 1, 512))
 
 

time: 106 us -> 106 us (level)
  transfers between devices with their start and end apart: 2 -> 2, of which waited for: 2 -> 2; matrix products, arithmetic and copies ran while one was open for 0% -> 0% of each run, Pallas kernels for 0% -> 1%
where the time goes in v6:
time: 106 us
  blocking collectives  74.2 us (70%)
  Pallas kernels  18.4 us (17%)
  starting transfers between devices  9.38 us (9%)
  waiting for transfers between devices  1.51 us (1%)
  local copies, waits for them, and re-layouts  1.28 us (1%)
    all_to_all x1, blocking collectives, total_sum(): lax.all_to_all(jnp.broadcast_to(own, (8, 5, 4, LANES)), FAR, 0, 0, tiled=...  25.6 us
    all_to_all x1, blocking collectives, per_device(): lax.all_to_all(split_columns(tensor), ('y', 'core'), 0, 0, tiled=True)  24.4 us
    pallas_call x1, Pallas kernels, chain(): pl.pallas_call(chain_kernel, out_shape=(jax.ShapeDtypeStruct((512, 512),...  15.8 us
    all_to_all x1, blocking collectives, total_sum(): lax.all_to_all(jnp.broadcast_to(own, (32, 5, 4, LANES)), NEAR, 0, 0, tile...  12.8 us
    all_to_all x1, blocking collectives, total_sum(): own = lax.all_to_all(own, NEAR, 0, 0, tiled=True).sum(0)  11.5 us
    ppermute x2, starting transfers between devices, swap_cores(): return lax.ppermute(x, 'core', [(0, 1), (1, 0)])  9.38 us
  transfers between devices with their start and end apart: 2, of which 2 were waited for; matrix products, arithmetic and copies ran while one was open for 0% of the time, Pallas kernels for 1%

profile of v6, /device:TPU:1, one launch (start us, length us, event | category | flops | bytes accessed | tf_op | source)
XLA Modules:
  0.0 105.6 jit_solution(16849397110560993112)
XLA Ops:
  0.6 0.0 copy-start
  0.6 1.2 %copy-done = f32[64,1,4096]{2,1,0:T(1,128)S(1)} copy-done((f32[64,1,4096]{2,1,0:T(1,128)S(1)}, f32[64,1,4096]{2,1,0:T(1,128)}, u32[]{:S(2)}) %copy-start) | copy-done | bytes 1048600
  1.9 0.6 shard_map.49
  2.5 24.4 %all_to_all.20 = f32[8,64,512]{2,1,0:T(8,128)S(1)} all-to-all(f32[8,64,512]{2,1,0:T(8,128)S(1)} %shard_map.49), channel_id=1, replica_groups=mesh['y'=4,'core'=2,'z_high'=8,'z_low'=2,'x'=4] {'y','core'}, dimensions={0} | all-to-all | bytes 2097152 | tf_op jit(solution)/shard_map/all_to_all | solution.py:313
  26.8 1.0 shard_map.51
  27.8 2.9 %collective-permute-start = (f32[640,128]{1,0:T(8,128)S(1)}, f32[640,128]{1,0:T(8,128)S(1)}, u32[]{:S(2)}, u32[]{:S(2)}) collective-permute-start(f32[640,128]{1,0:T(8,128)S(1)} %shard_map.51), channel_id=1, source_target_pairs={{0,64},{64,0},{1,65},{65,1},{2,66},{66,2},{3,67},{67,3},{4,68},{68... | collective-permute-start | bytes 983048 | tf_op jit(solution)/shard_map/ppermute | solution.py:299
  30.7 1.0 shard_map.50
  31.7 0.3 collective-permute-done
  32.0 11.5 %all_to_all.21 = f32[32,5,4,128]{3,2,1,0:T(4,128)S(1)} all-to-all(f32[32,5,4,128]{3,2,1,0:T(4,128)S(1)} %bitcast.11), channel_id=1, replica_groups=mesh['y'=4,'core'=2,'z_high'=8,'z_low'=2,'x'=4] {'y','z_low','x'}, dimensions={0} | all-to-all | bytes 655360 | tf_op jit(solution)/shard_map/all_to_all | solution.py:305
  43.5 0.1 reduce_sum.18
  43.6 25.6 %all_to_all.22 = f32[8,5,4,128]{3,2,1,0:T(4,128)S(1)} all-to-all(f32[8,5,4,128]{3,2,1,0:T(4,128)S(1)} %broadcast_in_dim.6), channel_id=1, replica_groups=mesh['y'=4,'core'=2,'z_high'=8,'z_low'=2,'x'=4] {'z_high'}, dimensions={0} | all-to-all | bytes 163840 | tf_op jit(solution)/shard_map/all_to_all | solution.py:306
  69.2 0.0 copy-start.1
  69.2 12.8 %all_to_all.23 = f32[32,5,4,128]{3,2,1,0:T(4,128)S(1)} all-to-all(f32[32,5,4,128]{3,2,1,0:T(4,128)S(1)} %broadcast_in_dim.7), channel_id=1, replica_groups=mesh['y'=4,'core'=2,'z_high'=8,'z_low'=2,'x'=4] {'y','z_low','x'}, dimensions={0} | all-to-all | bytes 655360 | tf_op jit(solution)/shard_map/all_to_all | solution.py:307
  82.1 6.4 %collective-permute-start.1 = (f32[640,128]{1,0:T(8,128)S(1)}, f32[640,128]{1,0:T(8,128)S(1)}, u32[]{:S(2)}, u32[]{:S(2)}) collective-permute-start(f32[640,128]{1,0:T(8,128)S(1)} %bitcast.8), channel_id=1, source_target_pairs={{0,64},{64,0},{1,65},{65,1},{2,66},{66,2},{3,67},{67,3},{4,68},{68... | collective-permute-start | bytes 983048 | tf_op jit(solution)/shard_map/ppermute | solution.py:299
  88.5 1.2 %collective-permute-done.1.other_ref = f32[640,128]{1,0:T(8,128)S(1)} collective-permute-done((f32[640,128]{1,0:T(8,128)S(1)}, f32[640,128]{1,0:T(8,128)S(1)}, u32[]{:S(2)}, u32[]{:S(2)}) %collective-permute-start.1) | collective-permute-done | bytes 327712 | tf_op jit(solution)/shard_map/ppermute | solution.py:299
  89.8 0.0 copy-done.1
  89.8 15.8 %shard_map.52 = (f32[512,512]{1,0:T(8,128)}, f32[512,128]{1,0:T(8,128)}, f32[512,128]{1,0:T(8,128)}) custom-call(f32[640,128]{1,0:T(8,128)S(1)} %bitcast.9, f32[640,128]{1,0:T(8,128)S(1)} %collective-permute-done.1.other_ref, f32[512,128]{1,0:T(8,128)S(1)} %copy-done.1, f32[512,512]{1,0:T(8,128)S(1)} %bitcast.7), custom_call_target="tpu_custom_call" | custom-call | tf_op jit(solution)/shard_map/pallas_call | solution.py:227
  (4 shorter events, 0.1 us)
Async XLA Ops:
  0.6 1.2 %copy-start = (f32[64,1,4096]{2,1,0:T(1,128)S(1)}, f32[64,1,4096]{2,1,0:T(1,128)}, u32[]{:S(2)}) copy-start(f32[64,1,4096]{2,1,0:T(1,128)} %param.2) | copy-start | bytes 3145732
  27.8 4.2 %collective-permute-start = (f32[640,128]{1,0:T(8,128)S(1)}, f32[640,128]{1,0:T(8,128)S(1)}, u32[]{:S(2)}, u32[]{:S(2)}) collective-permute-start(f32[640,128]{1,0:T(8,128)S(1)} %shard_map.51), channel_id=1, source_target_pairs={{0,64},{64,0},{1,65},{65,1},{2,66},{66,2},{3,67},{67,3},{4,68},{68... | collective-permute-start | bytes 983048 | tf_op jit(solution)/shard_map/ppermute | solution.py:299
  69.2 20.5 %copy-start.1 = (f32[512,128]{1,0:T(8,128)S(1)}, f32[512,128]{1,0:T(8,128)}, u32[]{:S(2)}) copy-start(f32[512,128]{1,0:T(8,128)} %x_ref.1) | copy-start | bytes 786436
  82.1 7.7 %collective-permute-start.1 = (f32[640,128]{1,0:T(8,128)S(1)}, f32[640,128]{1,0:T(8,128)S(1)}, u32[]{:S(2)}, u32[]{:S(2)}) collective-permute-start(f32[640,128]{1,0:T(8,128)S(1)} %bitcast.8), channel_id=1, source_target_pairs={{0,64},{64,0},{1,65},{65,1},{2,66},{66,2},{3,67},{67,3},{4,68},{68... | collective-permute-start | bytes 983048 | tf_op jit(solution)/shard_map/ppermute | solution.py:299

commit v7 on v5

--- a/solution.py
+++ b/solution.py
@@ -10,7 +10,7 @@
 LANES = 128
 BLOCKS = [(r, c) for r in range(4) for c in range(r + 1)]
 HALF = len(BLOCKS) // 2
-NEAR = ("y", "z_low", "x")
+NEAR = ("x", "z_low", "y")
 FAR = ("z_high",)
 PER_F, PER_B = (2, 2, 2, 2), 1
 

time: 106 us -> 106 us (level)
  no operation moved by 1% of the time
where the time goes in v7:
time: 106 us
  blocking collectives  73.8 us (70%)
  Pallas kernels  17.8 us (17%)
  starting transfers between devices  9.4 us (9%)
  waiting for transfers between devices  2.47 us (2%)
  local copies, waits for them, and re-layouts  1.28 us (1%)
    all_to_all x1, blocking collectives, total_sum(): lax.all_to_all(jnp.broadcast_to(own, (8, 5, 4, LANES)), FAR, 0, 0, tiled=...  25.9 us
    all_to_all x1, blocking collectives, per_device(): lax.all_to_all(split_columns(tensor), ('y', 'core'), 0, 0, tiled=True)  24.4 us
    pallas_call x1, Pallas kernels, chain(): pl.pallas_call(chain_kernel, out_shape=(jax.ShapeDtypeStruct((512, 512),...  15.8 us
    all_to_all x1, blocking collectives, total_sum(): lax.all_to_all(jnp.broadcast_to(own, (32, 5, 4, LANES)), NEAR, 0, 0, tile...  12.1 us
    all_to_all x1, blocking collectives, total_sum(): own = lax.all_to_all(own, NEAR, 0, 0, tiled=True).sum(0)  11.5 us
    ppermute x2, starting transfers between devices, swap_cores(): return lax.ppermute(x, 'core', [(0, 1), (1, 0)])  9.4 us
    ppermute x2, waiting for transfers between devices, swap_cores(): return lax.ppermute(x, 'core', [(0, 1), (1, 0)])  2.47 us
  transfers between devices with their start and end apart: 2, of which 2 were waited for; matrix products, arithmetic and copies ran while one was open for 0% of the time, Pallas kernels for 0%

profile of v7, /device:TPU:1, one launch (start us, length us, event | category | flops | bytes accessed | tf_op | source)
XLA Modules:
  0.0 105.6 jit_solution(1285516644622922028)
XLA Ops:
  0.6 0.0 copy-start
  0.6 1.2 %copy-done = f32[64,1,4096]{2,1,0:T(1,128)S(1)} copy-done((f32[64,1,4096]{2,1,0:T(1,128)S(1)}, f32[64,1,4096]{2,1,0:T(1,128)}, u32[]{:S(2)}) %copy-start) | copy-done | bytes 1048600
  1.9 0.6 shard_map.49
  2.5 24.4 %all_to_all.20 = f32[8,64,512]{2,1,0:T(8,128)S(1)} all-to-all(f32[8,64,512]{2,1,0:T(8,128)S(1)} %shard_map.49), channel_id=1, replica_groups=mesh['y'=4,'core'=2,'z_high'=8,'z_low'=2,'x'=4] {'y','core'}, dimensions={0} | all-to-all | bytes 2097152 | tf_op jit(solution)/shard_map/all_to_all | solution.py:307
  26.8 1.4 %shard_map.50 = (f32[640,128]{1,0:T(8,128)S(1)}, f32[640,128]{1,0:T(8,128)S(1)}) custom-call(f32[512,512]{1,0:T(8,128)S(1)} %bitcast.5), custom_call_target="tpu_custom_call" | custom-call | tf_op jit(solution)/shard_map/pallas_call | solution.py:288
  28.2 2.9 %collective-permute-start = (f32[640,128]{1,0:T(8,128)S(1)}, f32[640,128]{1,0:T(8,128)S(1)}, u32[]{:S(2)}, u32[]{:S(2)}) collective-permute-start(f32[640,128]{1,0:T(8,128)S(1)} %get-tuple-element.9), channel_id=1, source_target_pairs={{0,64},{64,0},{1,65},{65,1},{2,66},{66,2},{3,67},{67,3},{4,68},{68... | collective-permute-start | bytes 983048 | tf_op jit(solution)/shard_map/ppermute | solution.py:294
  31.1 1.2 %collective-permute-done = f32[640,128]{1,0:T(8,128)S(1)} collective-permute-done((f32[640,128]{1,0:T(8,128)S(1)}, f32[640,128]{1,0:T(8,128)S(1)}, u32[]{:S(2)}, u32[]{:S(2)}) %collective-permute-start) | collective-permute-done | bytes 327712 | tf_op jit(solution)/shard_map/ppermute | solution.py:294
  32.4 11.5 %all_to_all.21 = f32[32,5,4,128]{3,2,1,0:T(4,128)S(1)} all-to-all(f32[32,5,4,128]{3,2,1,0:T(4,128)S(1)} %bitcast.10), channel_id=1, replica_groups=mesh['y'=4,'core'=2,'z_high'=8,'z_low'=2,'x'=4] {'x','z_low','y'}, dimensions={0} | all-to-all | bytes 655360 | tf_op jit(solution)/shard_map/all_to_all | solution.py:299
  43.9 0.1 reduce_sum.18
  44.0 25.9 %all_to_all.22 = f32[8,5,4,128]{3,2,1,0:T(4,128)S(1)} all-to-all(f32[8,5,4,128]{3,2,1,0:T(4,128)S(1)} %broadcast_in_dim.6), channel_id=1, replica_groups=mesh['y'=4,'core'=2,'z_high'=8,'z_low'=2,'x'=4] {'z_high'}, dimensions={0} | all-to-all | bytes 163840 | tf_op jit(solution)/shard_map/all_to_all | solution.py:300
  70.0 0.0 copy-start.1
  70.0 12.1 %all_to_all.23 = f32[32,5,4,128]{3,2,1,0:T(4,128)S(1)} all-to-all(f32[32,5,4,128]{3,2,1,0:T(4,128)S(1)} %broadcast_in_dim.7), channel_id=1, replica_groups=mesh['y'=4,'core'=2,'z_high'=8,'z_low'=2,'x'=4] {'x','z_low','y'}, dimensions={0} | all-to-all | bytes 655360 | tf_op jit(solution)/shard_map/all_to_all | solution.py:301
  82.0 6.5 %collective-permute-start.1 = (f32[640,128]{1,0:T(8,128)S(1)}, f32[640,128]{1,0:T(8,128)S(1)}, u32[]{:S(2)}, u32[]{:S(2)}) collective-permute-start(f32[640,128]{1,0:T(8,128)S(1)} %bitcast.7), channel_id=1, source_target_pairs={{0,64},{64,0},{1,65},{65,1},{2,66},{66,2},{3,67},{67,3},{4,68},{68... | collective-permute-start | bytes 983048 | tf_op jit(solution)/shard_map/ppermute | solution.py:294
  88.5 1.2 %collective-permute-done.1.other_ref = f32[640,128]{1,0:T(8,128)S(1)} collective-permute-done((f32[640,128]{1,0:T(8,128)S(1)}, f32[640,128]{1,0:T(8,128)S(1)}, u32[]{:S(2)}, u32[]{:S(2)}) %collective-permute-start.1) | collective-permute-done | bytes 327712 | tf_op jit(solution)/shard_map/ppermute | solution.py:294
  89.7 0.0 copy-done.1
  89.7 15.8 %shard_map.51 = (f32[512,512]{1,0:T(8,128)}, f32[512,128]{1,0:T(8,128)}, f32[512,128]{1,0:T(8,128)}) custom-call(f32[640,128]{1,0:T(8,128)S(1)} %bitcast.8, f32[640,128]{1,0:T(8,128)S(1)} %collective-permute-done.1.other_ref, f32[512,128]{1,0:T(8,128)S(1)} %copy-done.1, f32[512,512]{1,0:T(8,128)S(1)} %bitcast.6), custom_call_target="tpu_custom_call" | custom-call | tf_op jit(solution)/shard_map/pallas_call | solution.py:227
  (4 shorter events, 0.1 us)
Async XLA Ops:
  0.6 1.2 %copy-start = (f32[64,1,4096]{2,1,0:T(1,128)S(1)}, f32[64,1,4096]{2,1,0:T(1,128)}, u32[]{:S(2)}) copy-start(f32[64,1,4096]{2,1,0:T(1,128)} %param.2) | copy-start | bytes 3145732
  28.2 4.2 %collective-permute-start = (f32[640,128]{1,0:T(8,128)S(1)}, f32[640,128]{1,0:T(8,128)S(1)}, u32[]{:S(2)}, u32[]{:S(2)}) collective-permute-start(f32[640,128]{1,0:T(8,128)S(1)} %get-tuple-element.9), channel_id=1, source_target_pairs={{0,64},{64,0},{1,65},{65,1},{2,66},{66,2},{3,67},{67,3},{4,68},{68... | collective-permute-start | bytes 983048 | tf_op jit(solution)/shard_map/ppermute | solution.py:294
  70.0 19.8 %copy-start.1 = (f32[512,128]{1,0:T(8,128)S(1)}, f32[512,128]{1,0:T(8,128)}, u32[]{:S(2)}) copy-start(f32[512,128]{1,0:T(8,128)} %x_ref.1) | copy-start | bytes 786436
  82.0 7.7 %collective-permute-start.1 = (f32[640,128]{1,0:T(8,128)S(1)}, f32[640,128]{1,0:T(8,128)S(1)}, u32[]{:S(2)}, u32[]{:S(2)}) collective-permute-start(f32[640,128]{1,0:T(8,128)S(1)} %bitcast.7), channel_id=1, source_target_pairs={{0,64},{64,0},{1,65},{65,1},{2,66},{66,2},{3,67},{67,3},{4,68},{68... | collective-permute-start | bytes 983048 | tf_op jit(solution)/shard_map/ppermute | solution.py:294
